TPU v7x, 512 devices: a whole 4x8x8 slice. The times are simulated.
512 devices in a mesh: owner: 32 (over x, z_hi, core), panel: 16 (over z_lo, y).
Axes of the slice: x: 4, y: 8, z: 8 (z_hi: 4, z_lo: 2; z = z_hi * 2 + z_lo), core: 2. Of those that a mesh axis runs over, the one named last changes fastest.
Arguments:
- embeddings: bfloat16 [114688, 1024], P(('owner', 'panel')), may hold values from -256 to 256
- cluster_id: int32 [114688], P(('owner', 'panel')), may hold values from 0 to 511, as said below
- row_index: int32 [114688], P(('owner', 'panel')), may hold values from 0 to 114687, each once
Outputs:
- best_match: float32 [114688], P(('owner', 'panel'))
Inputs may be any that keep to these rules, and one draw needn't show every extreme that they name: `cluster_id`: in each aligned block of 224 rows, at most 14 rows have cluster ids with one same remainder modulo 32, and in every block some remainder has exactly 14 rows. `row_index`: each global index appears once.
All inputs are finite; a program needn't handle non-finite values.
Results may differ from a plain program's by a relative error of at most 0.00048.
Values may be sent and summed in bfloat16 or wider, within the bound.
A program may use at most 64 MiB of HBM per device.

v0:
```python
import jax
import jax.numpy as jnp
from jax import lax
from jax.sharding import PartitionSpec as P


def similarity(left_rows, right_rows):
    return lax.dot_general(
        left_rows, right_rows, (((1,), (1,)), ((), ())), preferred_element_type=jnp.float32
    )


def row_maxima(scores, left_keys, right_keys, row_total):
    cluster_base = left_keys // row_total * row_total
    allowed = (
        (right_keys[None, :] >= cluster_base[:, None])
        & (right_keys[None, :] < left_keys[:, None])
        & (left_keys[:, None] >= 0)
    )
    return jnp.max(jnp.where(allowed, scores, jnp.float32(-1.0)), axis=1)


def per_device(embeddings, cluster_id, row_index):
    row_count = embeddings.shape[0]
    owners = lax.axis_size("owner")
    panels = lax.axis_size("panel")
    row_total = row_count * owners * panels
    capacity = 2 * row_count // owners
    widened = embeddings.astype(jnp.float32)
    square_sum = jnp.sum(widened * widened, axis=1, keepdims=True)
    inverse_norm = lax.rsqrt(square_sum + 1e-06)
    unit_rows = (widened * inverse_norm).astype(jnp.bfloat16)
    row_keys = cluster_id * row_total + row_index
    owner_of = cluster_id % owners
    one_hot = (owner_of[:, None] == jnp.arange(owners, dtype=jnp.int32)[None, :]).astype(jnp.int32)
    slot_rank = jnp.sum(jnp.cumsum(one_hot, axis=0) * one_hot, axis=1) - 1
    slot_of = owner_of * capacity + slot_rank
    send_rows = (
        jnp.zeros((owners * capacity, embeddings.shape[1]), jnp.bfloat16).at[slot_of].set(unit_rows)
    )
    send_keys = jnp.full((owners * capacity,), -1, jnp.int32).at[slot_of].set(row_keys)
    local_rows, local_keys = (
        lax.all_to_all(send_rows, "owner", split_axis=0, concat_axis=0, tiled=True),
        lax.all_to_all(send_keys, "owner", split_axis=0, concat_axis=0, tiled=True),
    )
    local_count = local_rows.shape[0]
    start_best = jnp.full((local_count,), -1.0, jnp.float32)
    running = start_best
    piece_rows = lax.all_gather(local_rows, "panel", axis=0, tiled=True)
    piece_keys = lax.all_gather(local_keys, "panel", axis=0, tiled=True)
    piece_count = piece_rows.shape[0]
    block_count = max(piece_count // local_count, 1)
    block_width = piece_count // block_count

    def one_block(carried, block_pair):
        block_rows, block_keys = block_pair
        scores = similarity(local_rows, block_rows)
        return (jnp.maximum(carried, row_maxima(scores, local_keys, block_keys, row_total)), None)

    running, unused = lax.scan(
        one_block,
        running,
        (
            piece_rows.reshape(block_count, block_width, -1),
            piece_keys.reshape(block_count, block_width),
        ),
    )
    stored = lax.all_to_all(running, "owner", split_axis=0, concat_axis=0, tiled=True)
    return stored[slot_of]


def solution(mesh):
    placed = (P(("owner", "panel"), None), P(("owner", "panel")), P(("owner", "panel")))
    return jax.shard_map(
        per_device, mesh=mesh, in_specs=placed, out_specs=P(("owner", "panel")), check_vma=False
    )
```

profile of v0, /device:TPU:1, one launch (start us, length us, event | category | flops | bytes accessed | tf_op | source)
XLA Modules:
  0.0 288.7 jit_solution(583883924052552646)
XLA Ops:
  6.5 0.0 all-gather.2.cloned.1.call-start
  6.5 0.7 multiply_add_fusion
  7.3 0.6 reduce-window.6
  7.9 0.2 slice_reduce_fusion
  8.1 0.1 bitcast_bitcast_fusion
  8.2 1.2 fusion.7
  9.4 2.4 scatter_custom_fusion.1
  11.8 0.3 all_to_all.27
  12.1 39.2 %all_to_all.36 = bf16[32,14,1024]{2,1,0:T(8,128)(2,1)S(1)} all-to-all(bf16[32,14,1024]{2,1,0:T(8,128)(2,1)S(1)} %all_to_all.27), channel_id=1, replica_groups=mesh['owner'=32,'panel'=16] {'owner'}, dimensions={0} | all-to-all | bytes 1835008 | tf_op jit(solution)/shard_map/all_to_all | solution.py:43
  51.2 1.2 all_to_all.29
  52.4 0.0 all-gather.2.cloned.1.call-update
  52.4 1.3 scatter_custom_fusion
  53.7 0.7 all_to_all.24
  54.5 8.4 %all-to-all-start = ((s32[32,14,1]{1,2,0:T(1,128)}), s32[32,14,1]{1,2,0:T(1,128)S(1)}, u32[]{:S(2)}, u32[]{:S(2)}) async-start(s32[32,14,1]{1,2,0:T(1,128)} %bitcast.1), calls=%async_computation | async-start | bytes 32768 | tf_op jit(solution)/shard_map/all_to_all | solution.py:44
  62.9 1.3 dynamic-slice
  64.7 7.5 %all-to-all-done = s32[32,14,1]{1,2,0:T(1,128)S(1)} async-done(((s32[32,14,1]{1,2,0:T(1,128)}), s32[32,14,1]{1,2,0:T(1,128)S(1)}, u32[]{:S(2)}, u32[]{:S(2)}) %all-to-all-start) | async-done | bytes 1824 | tf_op jit(solution)/shard_map/all_to_all | solution.py:44
  72.2 0.5 broadcast.123
  72.7 0.7 sign_reduce_fusion
  73.4 0.1 reshape.97
  73.6 0.3 dynamic-update-slice
  73.8 58.2 %all-reduce.1 = s32[7168]{0:T(1024)S(1)} all-reduce(s32[7168]{0:T(1024)S(1)} %dynamic-update-slice), channel_id=1, replica_groups=mesh['owner'=32,'panel'=16] {'panel'}, use_global_device_ids=true, to_apply=%add.1 | all-reduce | flops 7168 | bytes 57344
  132.1 0.1 reshape.67
  132.1 0.1 sign.21
  132.3 88.8 %all-gather.2.cloned.1.call-done = bf16[7168,1024]{1,0:T(8,128)(2,1)} async-done(((bf16[448,1024]{1,0:T(8,128)(2,1)}), bf16[7168,1024]{1,0:T(8,128)(2,1)}) %all-gather.2.cloned.1.call-update) | async-done | bytes 14680080 | tf_op jit(solution)/shard_map/all_gather | solution.py:49
  221.1 37.2 %while.13 = (s32[]{:T(128)}, f32[448]{0:T(512)S(1)}, s32[16,448]{1,0:T(8,128)S(1)}, s32[448,1]{0,1:T(1,128)S(1)}, s32[448]{0:T(512)S(1)}, /*index=5*/bf16[16,448...) while((s32[]{:T(128)}, f32[448]{0:T(512)S(1)}, s32[16,448]{1,0:T(8,128)S(1)}, ...), condition=%wide.region_8.9_spmd.clone, body=%wide.region_6.8_spmd.clone.sunk | while | flops 412250496 | bytes 1860715 | solution.py:60
  221.1 2.2 fusion.25
  223.4 2.2 fusion.25
  225.8 2.2 fusion.25
  228.1 2.2 fusion.25
  230.4 2.2 fusion.25
  232.7 2.2 fusion.25
  235.1 2.2 fusion.25
  237.4 2.2 fusion.25
  239.7 2.2 fusion.25
  242.0 2.2 fusion.25
  244.4 2.2 fusion.25
  246.7 2.2 fusion.25
  249.0 2.2 fusion.25
  251.3 2.2 fusion.25
  253.6 2.2 fusion.25
  256.0 2.2 fusion.25
  258.2 0.7 all_to_all.30
  258.9 9.7 %all-to-all-start.2 = ((f32[32,14,1]{1,2,0:T(1,128)}), f32[32,14,1]{1,2,0:T(1,128)S(1)}, u32[]{:S(2)}, u32[]{:S(2)}) async-start(f32[32,14,1]{1,2,0:T(1,128)} %bitcast.4), calls=%async_computation.2 | async-start | bytes 32768 | tf_op jit(solution)/shard_map/all_to_all | solution.py:68
  268.7 9.3 %all-to-all-done.2 = f32[32,14,1]{1,2,0:T(1,128)S(1)} async-done(((f32[32,14,1]{1,2,0:T(1,128)}), f32[32,14,1]{1,2,0:T(1,128)S(1)}, u32[]{:S(2)}, u32[]{:S(2)}) %all-to-all-start.2) | async-done | bytes 1824 | tf_op jit(solution)/shard_map/all_to_all | solution.py:68
  278.0 0.5 broadcast.124
  278.5 0.7 reduce.15
  279.2 0.1 all_to_all.32
  279.3 2.5 gather_fusion
  (90 shorter events, 1.2 us)
Async XLA Ops:
  6.5 214.5 %all-gather.2.cloned.1.call-start = ((), (), s32[]{:S(2)}) async-start(), calls=%async_computation.3 | async-start | bytes 15597568 | tf_op jit(solution)/shard_map/all_gather | solution.py:49
  54.5 17.8 %all-to-all-start = ((s32[32,14,1]{1,2,0:T(1,128)}), s32[32,14,1]{1,2,0:T(1,128)S(1)}, u32[]{:S(2)}, u32[]{:S(2)}) async-start(s32[32,14,1]{1,2,0:T(1,128)} %bitcast.1), calls=%async_computation | async-start | bytes 32768 | tf_op jit(solution)/shard_map/all_to_all | solution.py:44
  258.9 19.1 %all-to-all-start.2 = ((f32[32,14,1]{1,2,0:T(1,128)}), f32[32,14,1]{1,2,0:T(1,128)S(1)}, u32[]{:S(2)}, u32[]{:S(2)}) async-start(f32[32,14,1]{1,2,0:T(1,128)} %bitcast.4), calls=%async_computation.2 | async-start | bytes 32768 | tf_op jit(solution)/shard_map/all_to_all | solution.py:68
Sparse Core Ops, SparseCore 0:
  52.6 168.4 all-gather.1
where the time goes:
time: 290 us; the launch traced here: 289 us
  waiting for transfers between devices  106 us (37%)
  blocking collectives  97.4 us (34%)
  matrix products  35.4 us (12%)
  starting transfers between devices  18.1 us (6%)
  between operations  14.1 us (5%)
  local copies, waits for them, and re-layouts  9.97 us (3%)
  other arithmetic  7.4 us (3%)
    all_gather x1, waiting for transfers between devices, per_device(): piece_rows = lax.all_gather(local_rows, 'panel', axis=0, tiled=True)  88.8 us
    unnamed x1, blocking collectives  58.2 us
    all_to_all x1, blocking collectives, per_device(): lax.all_to_all(send_rows, 'owner', split_axis=0, concat_axis=0, tiled=True)  39.2 us
    dot_general x16, matrix products, similarity(): lax.dot_general(left_rows, right_rows, (((1,), (1,)), ((), ())), preferre...  35.4 us
    all_to_all x1, starting transfers between devices, per_device(): lax.all_to_all(running, 'owner', split_axis=0, concat_axis=0, tiled=True)  9.72 us
    all_to_all x1, waiting for transfers between devices, per_device(): lax.all_to_all(running, 'owner', split_axis=0, concat_axis=0, tiled=True)  9.33 us
    all_to_all x1, starting transfers between devices, per_device(): lax.all_to_all(send_keys, 'owner', split_axis=0, concat_axis=0, tiled=True)  8.4 us
    all_to_all x1, waiting for transfers between devices, per_device(): lax.all_to_all(send_keys, 'owner', split_axis=0, concat_axis=0, tiled=True)  7.47 us
  transfers between devices with their start and end apart: 3, of which 3 were waited for; matrix products, arithmetic and copies ran while one was open for 2% of the time, Pallas kernels for 0%

commit v1 on v0

v1 whole, which is shorter than its diff:
```python
import jax
import jax.numpy as jnp
from jax import lax
from jax.experimental import pallas as pl
from jax.experimental.pallas import tpu as pltpu
from jax.sharding import PartitionSpec as P

MESH = pl.DeviceIdType.MESH
NX, NY, NZ = 4, 8, 8
CAP = 14
SLOT = 16
NQ = NX
CHUNK = NZ * CAP
ROWS = 224
DIM = 1024
SPAN = 1 << 17
CLASSES = NX * NZ


def gray(v):
    return v ^ (v >> 1)


def eye(rows, lanes):
    return lax.broadcasted_iota(jnp.int32, (rows, lanes), 0) == lax.broadcasted_iota(
        jnp.int32, (rows, lanes), 1
    )


def column_of(row, rows):
    lanes = row.shape[1]
    zero = jnp.zeros((rows, lanes), row.dtype)
    spread = jnp.broadcast_to(row, (rows, lanes))
    return jnp.sum(jnp.where(eye(rows, lanes), spread, zero), axis=1, keepdims=True)


def contract_lanes(left, right):
    return lax.dot_general(
        left, right, (((1,), (1,)), ((), ())), preferred_element_type=jnp.float32
    )


def kernel(
    emb_ref, cid_ref, idx_ref, out_ref,
    unit, send, recv, held, query, keys, key_cols, clu_cols, scores, best_k, best_q,
    part_out, part_in, final, back,
    a2a_send, a2a_recv, y_send, y_recv, k_send, k_recv, p_send, p_recv, b_send, b_recv,
):
    owner = lax.axis_index("owner")
    panel = lax.axis_index("panel")
    x, zh, core = owner // 8, (owner // 2) % 4, owner % 2
    zl, y = panel // 8, panel % 8
    z = zh * 2 + zl

    def at(ax, ay, az, ac):
        return {"owner": (ax * 4 + az // 2) * 2 + ac, "panel": (az % 2) * 8 + ay}

    def along_y(step, ac):
        return at(x, (y + step + NY) % NY, z, ac)

    other = 1 - core
    ring = [along_y(s, core) for s in (-2, -1, 1, 2)] + [
        along_y(-2, other), along_y(0, other), along_y(2, other)
    ]

    barrier = pltpu.get_barrier_semaphore()

    def greet(k, carry):
        pl.semaphore_signal(
            barrier, inc=1, device_id=at((x + k // NZ) % NX, y, (z + k % NZ) % NZ, core),
            device_id_type=MESH,
        )
        return carry

    lax.fori_loop(1, CLASSES, greet, 0)
    for peer in ring:
        pl.semaphore_signal(barrier, inc=1, device_id=peer, device_id_type=MESH)

    wide = emb_ref[...].astype(jnp.float32)
    inverse = lax.rsqrt(jnp.sum(wide * wide, axis=1, keepdims=True) + 1e-06)
    unit[...] = (wide * inverse).astype(jnp.bfloat16)
    cid = cid_ref[...]
    residue = cid & (CLASSES - 1)
    quarter = gray(((residue >> 3) - x) & (NX - 1))
    offset = quarter * NZ + (((residue & 7) - z) & (NZ - 1))
    key = (cid >> 5) * SPAN + idx_ref[...] + 1
    offset_col = column_of(offset, ROWS)
    key_col = column_of(key, ROWS)
    first = lax.broadcasted_iota(jnp.int32, (ROWS, ROWS), 0)
    second = lax.broadcasted_iota(jnp.int32, (ROWS, ROWS), 1)
    equal = offset_col == offset
    rank = jnp.sum((equal & (first < second)).astype(jnp.int32), axis=0, keepdims=True)
    rank_col = jnp.sum((equal & (second < first)).astype(jnp.int32), axis=1, keepdims=True)
    lane = lax.broadcasted_iota(jnp.int32, (ROWS, 128), 1)
    digits = jnp.zeros((ROWS, 128), jnp.int32)
    for d, shift in enumerate((14, 7, 0)):
        digits = jnp.where(lane == SLOT * d + rank_col, (key_col >> shift) & 127, digits)
    digits = digits.astype(jnp.float32).astype(jnp.bfloat16)

    pl.semaphore_wait(barrier, CLASSES - 1 + len(ring))

    for q in range(NQ):
        slot = lax.broadcasted_iota(jnp.int32, (NZ * SLOT, ROWS), 0) + q * NZ * SLOT
        pick = (slot == offset * SLOT + rank).astype(jnp.float32).astype(jnp.bfloat16)
        pick_key = (slot == offset * SLOT + CAP).astype(jnp.float32).astype(jnp.bfloat16)
        rows = jnp.dot(pick, unit[...], preferred_element_type=jnp.float32)
        extra = jnp.dot(pick_key, digits, preferred_element_type=jnp.float32)
        base = q * NZ * SLOT
        send[base : base + NZ * SLOT, :] = rows.astype(jnp.bfloat16)
        send[base : base + NZ * SLOT, 0:128] = (rows[:, 0:128] + extra).astype(jnp.bfloat16)
        if q == 0:
            recv[0, 0:SLOT, :] = send[0:SLOT, :]

        def give(dz, carry, q=q, base=base):
            pltpu.make_async_remote_copy(
                src_ref=send.at[pl.ds(pl.multiple_of(base + dz * SLOT, SLOT), SLOT)],
                dst_ref=recv.at[q, pl.ds(pl.multiple_of(dz * SLOT, SLOT), SLOT)],
                send_sem=a2a_send,
                recv_sem=a2a_recv.at[q],
                device_id=at((x + gray(q)) % NX, y, (z + dz) % NZ, core),
                device_id_type=MESH,
            ).start()
            return carry

        lax.fori_loop(1 if q == 0 else 0, NZ, give, 0)

    def block(q, j):
        if j < 4:
            return held.at[q, pl.ds(j * CHUNK, CHUNK)]
        return query.at[q, pl.ds((j - 4) * 128, CHUNK)]

    def pass_on(q, j, peer, to):
        rows = pltpu.make_async_remote_copy(
            src_ref=block(q, j), dst_ref=block(q, to),
            send_sem=y_send.at[q, to], recv_sem=y_recv.at[q, to],
            device_id=peer, device_id_type=MESH,
        )
        names = pltpu.make_async_remote_copy(
            src_ref=keys.at[q, j], dst_ref=keys.at[q, to],
            send_sem=k_send.at[q, to], recv_sem=k_recv.at[q, to],
            device_id=peer, device_id_type=MESH,
        )
        rows.start()
        names.start()
        return rows, names

    copies = {}
    right, left = along_y(1, core), along_y(-1, core)

    def arrived(q, j):
        for copy in copies[q, j]:
            copy.wait_recv()

    slot_row = lax.broadcasted_iota(jnp.int32, (CHUNK, NZ * SLOT), 0)
    slot_col = lax.broadcasted_iota(jnp.int32, (CHUNK, NZ * SLOT), 1)
    source, place = slot_row // CAP, slot_row % CAP
    squeeze = (slot_col == source * SLOT + place).astype(jnp.float32).astype(jnp.bfloat16)
    key_rows = (slot_col == source * SLOT + CAP).astype(jnp.float32).astype(jnp.bfloat16)
    own_digit = (slot_col < 3 * SLOT) & (slot_col % SLOT == place)
    digit_sum = (
        lax.broadcasted_iota(jnp.int32, (8, 128), 1) // SLOT
        == lax.broadcasted_iota(jnp.int32, (8, 128), 0)
    ).astype(jnp.float32).astype(jnp.bfloat16)

    def own(q):
        if q == 0:
            landed = recv.at[0, pl.ds(SLOT, (NZ - 1) * SLOT)]
        else:
            landed = recv.at[q]
        pltpu.make_async_copy(landed, landed, a2a_recv.at[q]).wait()
        held[q, 2 * CHUNK : 3 * CHUNK, :] = jnp.dot(
            squeeze, recv[q], preferred_element_type=jnp.float32
        ).astype(jnp.bfloat16)
        spread = jnp.dot(key_rows, recv[q, :, 0:128], preferred_element_type=jnp.float32)
        spread = jnp.where(own_digit, spread, 0.0).astype(jnp.bfloat16)
        sums = contract_lanes(digit_sum, spread)
        value = sums[0:1] * 16384.0 + sums[1:2] * 128.0 + sums[2:3]
        keys[q, 2] = jnp.concatenate([value, jnp.zeros((1, 128 - CHUNK), jnp.float32)], axis=1)
        copies[q, 1] = pass_on(q, 2, right, 1)
        copies[q, 3] = pass_on(q, 2, left, 3)

    def forward(q):
        arrived(q, 1)
        copies[q, 0] = pass_on(q, 1, right, 0)
        arrived(q, 3)
        copies[q, 4] = pass_on(q, 3, left, 4)

    def far(q):
        arrived(q, 4)
        copies[q, 5] = pass_on(q, 4, along_y(0, other), 5)
        arrived(q, 0)

    def cluster_of(value):
        return jnp.floor((value - 1.0) * (1.0 / SPAN))

    def compare(q):
        arrived(q, 5)
        for j in range(5):
            column = column_of(keys[q, j], CHUNK)
            column = jnp.broadcast_to(column, (CHUNK, 128))
            key_cols[q, j * CHUNK : (j + 1) * CHUNK, :] = column
            clu_cols[q, j * CHUNK : (j + 1) * CHUNK, :] = cluster_of(column)

        def tile(t, carry):
            qk = jnp.where(t <= q, q, t - q - 1)
            qq = jnp.where(t <= q, t, q)
            right_rows = query[qq]
            scores[0 : 4 * CHUNK, :] = contract_lanes(held[qk], right_rows)
            scores[4 * CHUNK : 5 * CHUNK, :] = contract_lanes(query[qk, 0:CHUNK, :], right_rows)
            col_best = best_q[qq]
            halves = []
            for h in range(2):
                key_row = keys[qq, 4 + h]
                halves.append((key_row, cluster_of(key_row)))
            tops = [col_best[:, 0:128], col_best[:, 128:256]]
            for g in range(5 * CHUNK // 8):
                at_rows = pl.ds(g * 8, 8)
                key_col = key_cols[qk, at_rows, :]
                clu_col = clu_cols[qk, at_rows, :]
                top = best_k[qk, at_rows, :]
                for h in range(2):
                    key_row, clu_row = halves[h]
                    value = scores[at_rows, h * 128 : (h + 1) * 128]
                    value = jnp.where(clu_col == clu_row, value, -1.0)
                    top = jnp.maximum(top, jnp.where(key_row < key_col, value, -1.0))
                    tops[h] = jnp.maximum(tops[h], jnp.where(key_col < key_row, value, -1.0))
                best_k[qk, at_rows, :] = top
            best_q[qq, :, 0:128] = tops[0]
            best_q[qq, :, 128:256] = tops[1]
            return carry

        lax.fori_loop(0, 2 * q + 1, tile, 0)

    best_k[...] = jnp.full(best_k.shape, -1.0, jnp.float32)
    best_q[...] = jnp.full(best_q.shape, -1.0, jnp.float32)
    for q in range(NQ):
        for h in range(2):
            query[q, h * 128 + CHUNK : (h + 1) * 128, :] = jnp.zeros((128 - CHUNK, DIM), jnp.bfloat16)

    own(0)
    own(1)
    forward(0)
    own(2)
    forward(1)
    far(0)
    own(3)
    forward(2)
    far(1)
    compare(0)
    forward(3)
    far(2)
    compare(1)
    far(3)
    compare(2)
    compare(3)

    square = eye(CHUNK, 128)
    for q in range(NQ):
        for j in range(5):
            column = jnp.max(best_k[q, j * CHUNK : (j + 1) * CHUNK, :], axis=1, keepdims=True)
            row = jnp.max(
                jnp.where(square, jnp.broadcast_to(column, (CHUNK, 128)), -1.0), axis=0, keepdims=True
            )
            if j == 4:
                row = jnp.maximum(row, jnp.max(best_q[q, :, 0:128], axis=0, keepdims=True))
            part_out[j, q : q + 1, :] = row
        part_out[5, q : q + 1, :] = jnp.max(best_q[q, :, 128:256], axis=0, keepdims=True)
    parts = []
    for j, peer in (
        (0, along_y(-2, core)), (1, left), (3, right),
        (4, along_y(2, core)), (5, along_y(2, other)),
    ):
        part_out[j, 4:8, :] = jnp.full((4, 128), -1.0, jnp.float32)
        copy = pltpu.make_async_remote_copy(
            src_ref=part_out.at[j], dst_ref=part_in.at[j],
            send_sem=p_send.at[j], recv_sem=p_recv.at[j],
            device_id=peer, device_id_type=MESH,
        )
        copy.start()
        parts.append((j, copy))
    best = part_out[2, 0:NQ, :]
    for j, copy in parts:
        copy.wait_recv()
        best = jnp.maximum(best, part_in[j, 0:NQ, :])
    for q in range(NQ):
        final[q] = best[q : q + 1, :]
    back[0] = best[0:1, :]

    for q in range(NQ):

        def give_back(dz, carry, q=q):
            pltpu.make_async_remote_copy(
                src_ref=final.at[q],
                dst_ref=back.at[q * NZ + dz],
                send_sem=b_send,
                recv_sem=b_recv,
                device_id=at((x - gray(q) + NX) % NX, y, (z - dz + NZ) % NZ, core),
                device_id_type=MESH,
            ).start()
            return carry

        lax.fori_loop(1 if q == 0 else 0, NZ, give_back, 0)

    inbound = back.at[pl.ds(1, CLASSES - 1)]
    pltpu.make_async_copy(inbound, inbound, b_recv).wait()
    lane_row = lax.broadcasted_iota(jnp.int32, (1, 128), 1)
    spot = (offset & (NZ - 1)) * CAP + rank
    hit = lax.broadcasted_iota(jnp.int32, (128, ROWS), 0) == spot
    result = jnp.zeros((1, ROWS), jnp.float32)
    for q in range(NQ):
        mine = jnp.zeros((1, 128), jnp.float32)
        for dz in range(NZ):
            mine = jnp.where(lane_row // CAP == dz, back[q * NZ + dz], mine)
        column = jnp.broadcast_to(column_of(mine, 128), (128, ROWS))
        chosen = jnp.sum(jnp.where(hit, column, 0.0), axis=0, keepdims=True)
        result = jnp.where(offset >> 3 == q, chosen, result)
    out_ref[...] = result

    gone = send.at[pl.ds(SLOT, (CLASSES - 1) * SLOT)]
    pltpu.make_async_copy(gone, gone, a2a_send).wait()
    for pair in copies.values():
        for copy in pair:
            copy.wait_send()
    for j, copy in parts:
        copy.wait_send()
    pltpu.make_async_copy(inbound, inbound, b_send).wait()


def per_device(embeddings, cluster_id, row_index):
    vmem = pl.BlockSpec(memory_space=pltpu.VMEM)
    result = pl.pallas_call(
        kernel,
        out_shape=jax.ShapeDtypeStruct((1, ROWS), jnp.float32),
        in_specs=[vmem] * 3,
        out_specs=vmem,
        scratch_shapes=[
            pltpu.VMEM((ROWS, DIM), jnp.bfloat16),
            pltpu.VMEM((CLASSES * SLOT, DIM), jnp.bfloat16),
            pltpu.VMEM((NQ, NZ * SLOT, DIM), jnp.bfloat16),
            pltpu.VMEM((NQ, 4 * CHUNK, DIM), jnp.bfloat16),
            pltpu.VMEM((NQ, 256, DIM), jnp.bfloat16),
            pltpu.VMEM((NQ, 6, 1, 128), jnp.float32),
            pltpu.VMEM((NQ, 5 * CHUNK, 128), jnp.float32),
            pltpu.VMEM((NQ, 5 * CHUNK, 128), jnp.float32),
            pltpu.VMEM((5 * CHUNK, 256), jnp.float32),
            pltpu.VMEM((NQ, 5 * CHUNK, 128), jnp.float32),
            pltpu.VMEM((NQ, 8, 256), jnp.float32),
            pltpu.VMEM((6, 8, 128), jnp.float32),
            pltpu.VMEM((6, 8, 128), jnp.float32),
            pltpu.VMEM((NQ, 1, 128), jnp.float32),
            pltpu.VMEM((CLASSES, 1, 128), jnp.float32),
            pltpu.SemaphoreType.DMA,
            pltpu.SemaphoreType.DMA((NQ,)),
            pltpu.SemaphoreType.DMA((NQ, 6)),
            pltpu.SemaphoreType.DMA((NQ, 6)),
            pltpu.SemaphoreType.DMA((NQ, 6)),
            pltpu.SemaphoreType.DMA((NQ, 6)),
            pltpu.SemaphoreType.DMA((6,)),
            pltpu.SemaphoreType.DMA((6,)),
            pltpu.SemaphoreType.DMA,
            pltpu.SemaphoreType.DMA,
        ],
        compiler_params=pltpu.CompilerParams(
            collective_id=0, has_side_effects=True, vmem_limit_bytes=48 * 1024 * 1024
        ),
    )(embeddings, cluster_id.reshape(1, ROWS), row_index.reshape(1, ROWS))
    return result.reshape(ROWS)


def solution(mesh):
    placed = (P(("owner", "panel"), None), P(("owner", "panel")), P(("owner", "panel")))
    return jax.shard_map(
        per_device, mesh=mesh, in_specs=placed, out_specs=P(("owner", "panel")), check_vma=False
    )
```

time: 290 us -> 88.3 us (0.30)
  waiting for transfers between devices: 106 us -> 0 us
  blocking collectives: 97.4 us -> 0 us
  Pallas kernels: 0 us -> 85.8 us
  matrix products: 35.4 us -> 0 us
  starting transfers between devices: 18.1 us -> 0 us
  between operations: 14.1 us -> 0.01 us
  local copies, waits for them, and re-layouts: 9.97 us -> 2.28 us
  other arithmetic: 7.4 us -> 0 us
    all_gather x1 -> x0, waiting for transfers between devices: 88.8 us -> none  [per_device(): piece_rows = lax.all_gather(local_rows, 'panel', axis=0, tiled=True)]
    pallas_call x0 -> x1, Pallas kernels: none -> 85.8 us  [per_device(): pl.pallas_call(kernel, out_shape=jax.ShapeDtypeStruct((1, ROWS), jnp.floa...]
    unnamed x1 -> x0, blocking collectives: 58.2 us -> none
    all_to_all x1 -> x0, blocking collectives: 39.2 us -> none  [per_device(): lax.all_to_all(send_rows, 'owner', split_axis=0, concat_axis=0, tiled=True)]
    dot_general x16 -> x0, matrix products: 35.4 us -> none  [similarity(): lax.dot_general(left_rows, right_rows, (((1,), (1,)), ((), ())), preferre...]
    all_to_all x2 -> x0, starting transfers between devices: 18.1 us -> none  [the longest x1 9.72 us: per_device(): lax.all_to_all(running, 'owner', split_axis=0, concat_axis=0, tiled=True)]
    all_to_all x2 -> x0, waiting for transfers between devices: 16.8 us -> none  [the longest x1 9.33 us: per_device(): lax.all_to_all(running, 'owner', split_axis=0, concat_axis=0, tiled=True)]
    all_to_all x8 -> x0, local copies, waits for them, and re-layouts: 4.08 us -> none  [the longest x2 1.44 us: per_device(): lax.all_to_all(send_rows, 'owner', split_axis=0, concat_axis=0, tiled=True)]
  transfers between devices with their start and end apart: 3 -> 0, of which waited for: 3 -> 0; matrix products, arithmetic and copies ran while one was open for 2% -> 0% of each run, Pallas kernels for 0% -> 0%
where the time goes in v1:
time: 88.3 us; the launch traced here: 88.1 us
  Pallas kernels  85.8 us (97%)
  local copies, waits for them, and re-layouts  2.28 us (3%)
    pallas_call x1, Pallas kernels, per_device(): pl.pallas_call(kernel, out_shape=jax.ShapeDtypeStruct((1, ROWS), jnp.floa...  85.8 us
    unnamed x7, local copies, waits for them, and re-layouts  2.28 us

profile of v1, /device:TPU:1, one launch (start us, length us, event | category | flops | bytes accessed | tf_op | source)
XLA Modules:
  0.0 88.1 jit_solution(18255609470973523607)
XLA Ops:
  0.0 0.0 copy-start.2
  0.0 0.0 copy-start.1
  0.0 0.7 copy-done.2
  0.7 0.0 copy-done.1
  0.7 0.0 copy-start
  0.7 1.0 %copy-done = bf16[224,1024]{1,0:T(8,128)(2,1)S(1)} copy-done((bf16[224,1024]{1,0:T(8,128)(2,1)S(1)}, bf16[224,1024]{1,0:T(8,128)(2,1)}, u32[]{:S(2)}) %copy-start) | copy-done | bytes 458776
  1.7 85.8 %shard_map.37 = f32[1,224]{1,0:T(1,128)S(1)} custom-call(bf16[224,1024]{1,0:T(8,128)(2,1)S(1)} %copy-done, s32[1,224]{1,0:T(1,128)S(1)} %bitcast.4, s32[1,224]{1,0:T(1,128)S(1)} %bitcast.5), custom_call_target="tpu_custom_call" | custom-call | tf_op jit(solution)/shard_map/pallas_call | solution.py:331
  87.6 0.6 copy.5
Async XLA Ops:
  0.0 0.7 copy-start.2
  0.0 0.7 copy-start.1
  0.7 1.0 %copy-start = (bf16[224,1024]{1,0:T(8,128)(2,1)S(1)}, bf16[224,1024]{1,0:T(8,128)(2,1)}, u32[]{:S(2)}) copy-start(bf16[224,1024]{1,0:T(8,128)(2,1)} %emb_ref.1) | copy-start | bytes 1376260

commit v2 on v1

v2 whole, which is shorter than its diff:
```python
import jax
import jax.numpy as jnp
from jax import lax
from jax.experimental import pallas as pl
from jax.experimental.pallas import tpu as pltpu
from jax.sharding import PartitionSpec as P

MESH = pl.DeviceIdType.MESH
NX, NY, NZ = 4, 8, 8
CAP = 14
SLOT = 16
NQ = 4
PER = 8
CHUNK = PER * CAP
ROWS = 224
DIM = 1024
SPAN = 1 << 17
CLASSES = NQ * PER
HELD = 3 * CHUNK


def eye(rows, lanes):
    return lax.broadcasted_iota(jnp.int32, (rows, lanes), 0) == lax.broadcasted_iota(
        jnp.int32, (rows, lanes), 1
    )


def column_of(row, rows):
    lanes = row.shape[1]
    zero = jnp.zeros((rows, lanes), row.dtype)
    spread = jnp.broadcast_to(row, (rows, lanes))
    return jnp.sum(jnp.where(eye(rows, lanes), spread, zero), axis=1, keepdims=True)


def contract_lanes(left, right):
    return lax.dot_general(
        left, right, (((1,), (1,)), ((), ())), preferred_element_type=jnp.float32
    )


def to_bf16(mask):
    return mask.astype(jnp.float32).astype(jnp.bfloat16)


def y_steps(q, h):
    if q == 0:
        return 4 * h
    return q + h * (NY - 2 * q)


def kernel(
    emb_hbm, cid_hbm, idx_hbm, out_ref,
    emb_ref, cid_ref, idx_ref, unit, send, recv, held, query, keys, key_cols, clu_cols, scores,
    best_k, best_q, part_out, part_in, final, back,
    in_sem, a2a_send, a2a_recv, y_send, y_recv, k_send, k_recv, p_send, p_recv, b_send, b_recv,
):
    owner = lax.axis_index("owner")
    panel = lax.axis_index("panel")
    x, zh, core = owner // 8, (owner // 2) % 4, owner % 2
    zl, y = panel // 8, panel % 8
    z = zh * 2 + zl

    loads = [
        pltpu.make_async_copy(src, dst, in_sem.at[i])
        for i, (src, dst) in enumerate(
            ((cid_hbm, cid_ref), (idx_hbm, idx_ref), (emb_hbm, emb_ref))
        )
    ]
    for load in loads:
        load.start()

    def at(ax, ay, az, ac):
        return {"owner": (ax * 4 + az // 2) * 2 + ac, "panel": (az % 2) * 8 + ay}

    def along_x(step):
        return at((x + step + NX) % NX, y, z, core)

    def home(q, n):
        m = n % 4
        up = jnp.where((z + m) % 2 == 0, m, NZ - m)
        return at(x, (y + y_steps(q, n // 4)) % NY, (z + up) % NZ, core)

    def source(q, n):
        m = n % 4
        up = jnp.where(z % 2 == 0, NZ - m, m)
        return at(x, (y - y_steps(q, n // 4) + NY) % NY, (z + up) % NZ, core)

    pair_z = zh * 2 + 1 - zl
    pair, twin = at(x, y, pair_z, core), at(x, y, z, 1 - core)
    barrier = pltpu.get_barrier_semaphore()
    for q in range(NQ):

        def greet(n, carry, q=q):
            pl.semaphore_signal(barrier, inc=1, device_id=source(q, n), device_id_type=MESH)
            return carry

        lax.fori_loop(1 if q == 0 else 0, PER, greet, 0)
    nearby = [along_x(-1), along_x(1), pair, twin]
    for peer in nearby:
        pl.semaphore_signal(barrier, inc=1, device_id=peer, device_id_type=MESH)

    for load in loads[:2]:
        load.wait()
    cid = cid_ref[...]
    residue = cid & (CLASSES - 1)
    dy = ((residue >> 2) - y) & (NY - 1)
    quarter = jnp.where(dy == 4, 0, jnp.where(dy < 4, dy, NY - dy))
    half = (dy >= 4).astype(jnp.int32)
    dz = (z - 2 * (residue & 3)) & (NZ - 1)
    member = jnp.where((dz == 0) | (dz > 4), (NZ - dz) & (NZ - 1), dz - 1)
    place = half * 4 + member
    offset = quarter * PER + place
    key = (cid >> 5) * SPAN + idx_ref[...] + 1
    offset_col = column_of(offset, ROWS)
    key_col = column_of(key, ROWS)
    first = lax.broadcasted_iota(jnp.int32, (ROWS, ROWS), 0)
    second = lax.broadcasted_iota(jnp.int32, (ROWS, ROWS), 1)
    equal = offset_col == offset
    rank = jnp.sum((equal & (first < second)).astype(jnp.int32), axis=0, keepdims=True)
    rank_col = jnp.sum((equal & (second < first)).astype(jnp.int32), axis=1, keepdims=True)
    lane = lax.broadcasted_iota(jnp.int32, (ROWS, 128), 1)
    digits = jnp.zeros((ROWS, 128), jnp.int32)
    for d, shift in enumerate((14, 7, 0)):
        digits = jnp.where(lane == SLOT * d + rank_col, (key_col >> shift) & 127, digits)
    digits = digits.astype(jnp.float32).astype(jnp.bfloat16)

    loads[2].wait()
    wide = emb_ref[...].astype(jnp.float32)
    inverse = lax.rsqrt(jnp.sum(wide * wide, axis=1, keepdims=True) + 1e-06)
    unit[...] = (wide * inverse).astype(jnp.bfloat16)
    for q in range(NQ):
        base = q * PER * SLOT
        slot = lax.broadcasted_iota(jnp.int32, (PER * SLOT, ROWS), 0) + base
        pick = to_bf16(slot == offset * SLOT + rank)
        pick_key = to_bf16(slot == offset * SLOT + CAP)
        rows = jnp.dot(pick, unit[...], preferred_element_type=jnp.float32)
        extra = jnp.dot(pick_key, digits, preferred_element_type=jnp.float32)
        send[base : base + PER * SLOT, :] = rows.astype(jnp.bfloat16)
        send[base : base + PER * SLOT, 0:128] = (rows[:, 0:128] + extra).astype(jnp.bfloat16)
    recv[0, 0:SLOT, :] = send[0:SLOT, :]
    best_k[...] = jnp.full(best_k.shape, -1.0, jnp.float32)
    best_q[...] = jnp.full(best_q.shape, -1.0, jnp.float32)
    for q in range(NQ):
        for u in range(4):
            query[q, u * 128 + CHUNK : (u + 1) * 128, :] = jnp.zeros(
                (128 - CHUNK, DIM), jnp.bfloat16
            )

    pl.semaphore_wait(barrier, CLASSES - 1 + len(nearby))

    for q in range(NQ):

        def give(n, carry, q=q):
            start = pl.multiple_of(n * SLOT, SLOT)
            pltpu.make_async_remote_copy(
                src_ref=send.at[pl.ds(q * PER * SLOT + start, SLOT)],
                dst_ref=recv.at[q, pl.ds(start, SLOT)],
                send_sem=a2a_send,
                recv_sem=a2a_recv.at[q],
                device_id=home(q, n),
                device_id_type=MESH,
            ).start()
            return carry

        lax.fori_loop(1 if q == 0 else 0, PER, give, 0)

    def block(q, j):
        if j < 2:
            return held.at[q, pl.ds(j * CHUNK, CHUNK)]
        return query.at[q, pl.ds((j - 2) * 128, CHUNK)]

    copies = {}

    def pass_on(q, j, peer, to):
        rows = pltpu.make_async_remote_copy(
            src_ref=block(q, j), dst_ref=block(q, to),
            send_sem=y_send.at[q, to], recv_sem=y_recv.at[q, to],
            device_id=peer, device_id_type=MESH,
        )
        names = pltpu.make_async_remote_copy(
            src_ref=keys.at[q, j], dst_ref=keys.at[q, to],
            send_sem=k_send.at[q, to], recv_sem=k_recv.at[q, to],
            device_id=peer, device_id_type=MESH,
        )
        rows.start()
        names.start()
        copies[q, to] = rows, names

    def arrived(q, j):
        for copy in copies[q, j]:
            copy.wait_recv()

    slot_row = lax.broadcasted_iota(jnp.int32, (CHUNK, PER * SLOT), 0)
    slot_col = lax.broadcasted_iota(jnp.int32, (CHUNK, PER * SLOT), 1)
    sender, nth = slot_row // CAP, slot_row % CAP
    squeeze = to_bf16(slot_col == sender * SLOT + nth)
    key_rows = to_bf16(slot_col == sender * SLOT + CAP)
    own_digit = (slot_col < 3 * SLOT) & (slot_col % SLOT == nth)
    digit_sum = to_bf16(
        lax.broadcasted_iota(jnp.int32, (8, 128), 1) // SLOT
        == lax.broadcasted_iota(jnp.int32, (8, 128), 0)
    )

    def own(q):
        landed = recv.at[0, pl.ds(SLOT, (PER - 1) * SLOT)] if q == 0 else recv.at[q]
        pltpu.make_async_copy(landed, landed, a2a_recv.at[q]).wait()
        held[q, CHUNK : 2 * CHUNK, :] = jnp.dot(
            squeeze, recv[q], preferred_element_type=jnp.float32
        ).astype(jnp.bfloat16)
        spread = jnp.dot(key_rows, recv[q, :, 0:128], preferred_element_type=jnp.float32)
        spread = jnp.where(own_digit, spread, 0.0).astype(jnp.bfloat16)
        sums = contract_lanes(digit_sum, spread)
        value = sums[0:1] * 16384.0 + sums[1:2] * 128.0 + sums[2:3]
        keys[q, 1] = jnp.concatenate([value, jnp.zeros((1, 128 - CHUNK), jnp.float32)], axis=1)
        pass_on(q, 1, along_x(-1), 2)
        pass_on(q, 1, along_x(1), 0)

    def cross(q):
        arrived(q, 2)
        pass_on(q, 2, pair, 3)
        pass_on(q, 2, twin, 4)

    def share(q):
        arrived(q, 3)
        pass_on(q, 3, twin, 5)

    def cluster_of(value):
        return jnp.floor((value - 1.0) * (1.0 / SPAN))

    def near(q):
        arrived(q, 0)
        for j in range(3):
            column = jnp.broadcast_to(column_of(keys[q, j], CHUNK), (CHUNK, 128))
            key_cols[q, j * CHUNK : (j + 1) * CHUNK, :] = column
            clu_cols[q, j * CHUNK : (j + 1) * CHUNK, :] = cluster_of(column)

    def far(q):
        arrived(q, 4)
        arrived(q, 5)

    def tile(qk, qq):
        right_rows = query[qq]
        scores[0 : 2 * CHUNK, :] = contract_lanes(held[qk], right_rows)
        scores[2 * CHUNK : HELD, :] = contract_lanes(query[qk, 0:CHUNK, :], right_rows)
        key_row = [keys[qq, 2 + u] for u in range(4)]
        clu_row = [cluster_of(row) for row in key_row]
        tops = [best_q[qq, :, u * 128 : (u + 1) * 128] for u in range(4)]
        for g in range(HELD // 8):
            at_rows = slice(g * 8, g * 8 + 8)
            key_here = key_cols[qk, at_rows, :]
            clu_here = clu_cols[qk, at_rows, :]
            top = best_k[qk, at_rows, :]
            for u in range(4):
                value = scores[at_rows, u * 128 : (u + 1) * 128]
                value = jnp.where(clu_here == clu_row[u], value, -1.0)
                top = jnp.maximum(top, jnp.where(key_row[u] < key_here, value, -1.0))
                if CHUNK <= g * 8 < 2 * CHUNK:
                    tops[u] = jnp.maximum(tops[u], jnp.where(key_here < key_row[u], value, -1.0))
            best_k[qk, at_rows, :] = top
        for u in range(4):
            best_q[qq, :, u * 128 : (u + 1) * 128] = tops[u]

    def tiles(count, pick):
        def step(t, carry):
            tile(*pick(t))
            return carry

        lax.fori_loop(0, count, step, 0)

    def both_ways(q):
        return lambda t: (jnp.where(t <= q, q, t - q - 1), jnp.where(t <= q, t, q))

    own(0)
    own(1)
    cross(0)
    own(2)
    cross(1)
    share(0)
    near(0)
    cross(2)
    own(3)
    share(1)
    near(1)
    far(0)
    tiles(1, both_ways(0))
    share(2)
    far(1)
    tiles(3, both_ways(1))
    cross(3)
    near(2)
    far(2)
    near(3)
    tiles(5, both_ways(2))
    tiles(3, lambda t: (3, t))
    share(3)
    far(3)
    tiles(4, lambda t: (t, 3))

    square = eye(CHUNK, 128)

    def over_query(q, j):
        column = jnp.max(best_k[q, j * CHUNK : (j + 1) * CHUNK, :], axis=1, keepdims=True)
        column = jnp.broadcast_to(column, (CHUNK, 128))
        return jnp.max(jnp.where(square, column, -1.0), axis=0, keepdims=True)

    for q in range(NQ):
        for u in range(4):
            row = jnp.max(best_q[q, :, u * 128 : (u + 1) * 128], axis=0, keepdims=True)
            if u == 0:
                row = jnp.maximum(row, over_query(q, 2))
            part_out[u, q : q + 1, :] = row
        part_out[4, q : q + 1, :] = over_query(q, 0)
    parts = []
    ahead = (x + 1) % NX
    for u, peer in enumerate((
        at(ahead, y, z, core), at(ahead, y, pair_z, core),
        at(ahead, y, z, 1 - core), at(ahead, y, pair_z, 1 - core), along_x(-1),
    )):
        part_out[u, NQ:8, :] = jnp.full((8 - NQ, 128), -1.0, jnp.float32)
        copy = pltpu.make_async_remote_copy(
            src_ref=part_out.at[u], dst_ref=part_in.at[u],
            send_sem=p_send.at[u], recv_sem=p_recv.at[u],
            device_id=peer, device_id_type=MESH,
        )
        copy.start()
        parts.append(copy)
    best = [over_query(q, 1) for q in range(NQ)]
    for u, copy in enumerate(parts):
        copy.wait_recv()
        best = [jnp.maximum(best[q], part_in[u, q : q + 1, :]) for q in range(NQ)]
    for q in range(NQ):
        final[q] = best[q]
    back[0] = best[0]

    for q in range(NQ):

        def give_back(n, carry, q=q):
            pltpu.make_async_remote_copy(
                src_ref=final.at[q],
                dst_ref=back.at[q * PER + n],
                send_sem=b_send,
                recv_sem=b_recv,
                device_id=source(q, n),
                device_id_type=MESH,
            ).start()
            return carry

        lax.fori_loop(1 if q == 0 else 0, PER, give_back, 0)

    inbound = back.at[pl.ds(1, CLASSES - 1)]
    pltpu.make_async_copy(inbound, inbound, b_recv).wait()
    lane_row = lax.broadcasted_iota(jnp.int32, (1, 128), 1)
    hit = lax.broadcasted_iota(jnp.int32, (128, ROWS), 0) == place * CAP + rank
    result = jnp.zeros((1, ROWS), jnp.float32)
    for q in range(NQ):
        mine = jnp.zeros((1, 128), jnp.float32)
        for n in range(PER):
            mine = jnp.where(lane_row // CAP == n, back[q * PER + n], mine)
        column = jnp.broadcast_to(column_of(mine, 128), (128, ROWS))
        chosen = jnp.sum(jnp.where(hit, column, 0.0), axis=0, keepdims=True)
        result = jnp.where(quarter == q, chosen, result)
    out_ref[...] = result

    gone = send.at[pl.ds(SLOT, (CLASSES - 1) * SLOT)]
    pltpu.make_async_copy(gone, gone, a2a_send).wait()
    for both in copies.values():
        for copy in both:
            copy.wait_send()
    for copy in parts:
        copy.wait_send()
    pltpu.make_async_copy(inbound, inbound, b_send).wait()


def per_device(embeddings, cluster_id, row_index):
    result = pl.pallas_call(
        kernel,
        out_shape=jax.ShapeDtypeStruct((1, ROWS), jnp.float32),
        in_specs=[pl.BlockSpec(memory_space=pl.ANY)] * 3,
        out_specs=pl.BlockSpec(memory_space=pltpu.VMEM),
        scratch_shapes=[
            pltpu.VMEM((ROWS, DIM), jnp.bfloat16),
            pltpu.VMEM((1, ROWS), jnp.int32),
            pltpu.VMEM((1, ROWS), jnp.int32),
            pltpu.VMEM((ROWS, DIM), jnp.bfloat16),
            pltpu.VMEM((CLASSES * SLOT, DIM), jnp.bfloat16),
            pltpu.VMEM((NQ, PER * SLOT, DIM), jnp.bfloat16),
            pltpu.VMEM((NQ, 2 * CHUNK, DIM), jnp.bfloat16),
            pltpu.VMEM((NQ, 512, DIM), jnp.bfloat16),
            pltpu.VMEM((NQ, 6, 1, 128), jnp.float32),
            pltpu.VMEM((NQ, HELD, 128), jnp.float32),
            pltpu.VMEM((NQ, HELD, 128), jnp.float32),
            pltpu.VMEM((HELD, 512), jnp.float32),
            pltpu.VMEM((NQ, HELD, 128), jnp.float32),
            pltpu.VMEM((NQ, 8, 512), jnp.float32),
            pltpu.VMEM((5, 8, 128), jnp.float32),
            pltpu.VMEM((5, 8, 128), jnp.float32),
            pltpu.VMEM((NQ, 1, 128), jnp.float32),
            pltpu.VMEM((CLASSES, 1, 128), jnp.float32),
            pltpu.SemaphoreType.DMA((3,)),
            pltpu.SemaphoreType.DMA,
            pltpu.SemaphoreType.DMA((NQ,)),
            pltpu.SemaphoreType.DMA((NQ, 6)),
            pltpu.SemaphoreType.DMA((NQ, 6)),
            pltpu.SemaphoreType.DMA((NQ, 6)),
            pltpu.SemaphoreType.DMA((NQ, 6)),
            pltpu.SemaphoreType.DMA((5,)),
            pltpu.SemaphoreType.DMA((5,)),
            pltpu.SemaphoreType.DMA,
            pltpu.SemaphoreType.DMA,
        ],
        compiler_params=pltpu.CompilerParams(
            collective_id=0, has_side_effects=True, vmem_limit_bytes=48 * 1024 * 1024
        ),
    )(embeddings, cluster_id.reshape(1, ROWS), row_index.reshape(1, ROWS))
    return result.reshape(ROWS)


def solution(mesh):
    placed = (P(("owner", "panel"), None), P(("owner", "panel")), P(("owner", "panel")))
    return jax.shard_map(
        per_device, mesh=mesh, in_specs=placed, out_specs=P(("owner", "panel")), check_vma=False
    )
```

time: 88.3 us -> 80.3 us (0.909)
  Pallas kernels: 85.8 us -> 77.8 us
    pallas_call x1, Pallas kernels: 85.8 us -> 77.8 us  [per_device(): pl.pallas_call(kernel, out_shape=jax.ShapeDtypeStruct((1, ROWS), jnp.floa...]
where the time goes in v2:
time: 80.3 us; the launch traced here: 80.1 us
  Pallas kernels  77.8 us (97%)
  local copies, waits for them, and re-layouts  2.28 us (3%)
    pallas_call x1, Pallas kernels, per_device(): pl.pallas_call(kernel, out_shape=jax.ShapeDtypeStruct((1, ROWS), jnp.floa...  77.8 us
    unnamed x7, local copies, waits for them, and re-layouts  2.28 us

profile of v2, /device:TPU:1, one launch (start us, length us, event | category | flops | bytes accessed | tf_op | source)
XLA Modules:
  0.0 80.1 jit_solution(3945046972958594478)
XLA Ops:
  0.0 0.0 copy-start.2
  0.0 0.0 copy-start.1
  0.0 0.7 copy-done.2
  0.7 0.0 copy-done.1
  0.7 0.0 copy-start
  0.7 1.0 %copy-done = bf16[224,1024]{1,0:T(8,128)(2,1)S(1)} copy-done((bf16[224,1024]{1,0:T(8,128)(2,1)S(1)}, bf16[224,1024]{1,0:T(8,128)(2,1)}, u32[]{:S(2)}) %copy-start) | copy-done | bytes 458776
  1.7 77.8 %shard_map.37 = f32[1,224]{1,0:T(1,128)S(1)} custom-call(bf16[224,1024]{1,0:T(8,128)(2,1)S(1)} %copy-done, s32[1,224]{1,0:T(1,128)S(1)} %bitcast.4, s32[1,224]{1,0:T(1,128)S(1)} %bitcast.5), custom_call_target="tpu_custom_call" | custom-call | tf_op jit(solution)/shard_map/pallas_call | solution.py:375
  79.6 0.6 copy.5
Async XLA Ops:
  0.0 0.7 copy-start.2
  0.0 0.7 copy-start.1
  0.7 1.0 %copy-start = (bf16[224,1024]{1,0:T(8,128)(2,1)S(1)}, bf16[224,1024]{1,0:T(8,128)(2,1)}, u32[]{:S(2)}) copy-start(bf16[224,1024]{1,0:T(8,128)(2,1)} %emb_hbm.1) | copy-start | bytes 1376260

commit v3 on v2

v3 whole, which is shorter than its diff:
```python
import jax
import jax.numpy as jnp
from jax import lax
from jax.experimental import pallas as pl
from jax.experimental.pallas import tpu as pltpu
from jax.sharding import PartitionSpec as P

MESH = pl.DeviceIdType.MESH
NX, NY, NZ = 4, 8, 8
CAP = 14
SLOT = 16
NQ = 4
PER = 8
CHUNK = PER * CAP
ROWS = 224
DIM = 1024
SPAN = 1 << 17
CLASSES = NQ * PER
HELD = 3 * CHUNK


def eye(rows, lanes):
    return lax.broadcasted_iota(jnp.int32, (rows, lanes), 0) == lax.broadcasted_iota(
        jnp.int32, (rows, lanes), 1
    )


def column_of(row, rows):
    lanes = row.shape[1]
    zero = jnp.zeros((rows, lanes), row.dtype)
    spread = jnp.broadcast_to(row, (rows, lanes))
    return jnp.sum(jnp.where(eye(rows, lanes), spread, zero), axis=1, keepdims=True)


def contract_lanes(left, right):
    return lax.dot_general(
        left, right, (((1,), (1,)), ((), ())), preferred_element_type=jnp.float32
    )


def to_bf16(mask):
    return mask.astype(jnp.float32).astype(jnp.bfloat16)


def y_steps(n):
    return (n + 1) // 2 if n % 2 else (NY - n // 2) % NY


def z_steps(q):
    return (4 - q) % 4


FIRST = 48
FARTHEST = sorted(
    ((q, n) for q in range(NQ) for n in range(PER) if q or n),
    key=lambda slot: -(z_steps(slot[0]) + (slot[1] + 1) // 2),
)


def kernel(
    emb_hbm, cid_hbm, idx_hbm, out_ref,
    emb_ref, cid_ref, idx_ref, unit, send, recv, held, query, keys, key_cols, clu_cols, scores,
    best_k, best_q, part_out, part_in, final, back,
    in_sem, own_sem, a2a_send, a2a_recv, y_send, y_recv, k_send, k_recv, p_send, p_recv, b_send, b_recv,
):
    owner = lax.axis_index("owner")
    panel = lax.axis_index("panel")
    x, zh, core = owner // 8, (owner // 2) % 4, owner % 2
    zl, y = panel // 8, panel % 8
    z = zh * 2 + zl

    loads = [
        pltpu.make_async_copy(src, dst, in_sem.at[i])
        for i, (src, dst) in enumerate(
            ((cid_hbm, cid_ref), (idx_hbm, idx_ref), (emb_hbm, emb_ref))
        )
    ]
    for load in loads:
        load.start()

    def at(ax, ay, az, ac):
        return {"owner": (ax * 4 + az // 2) * 2 + ac, "panel": (az % 2) * 8 + ay}

    def along_x(step):
        return at((x + step + NX) % NX, y, z, core)

    def home(q, n):
        m = z_steps(q)
        up = jnp.where((z + m) % 2 == 0, m, NZ - m)
        return at(x, (y + y_steps(n)) % NY, (z + up) % NZ, core)

    def source(q, n):
        m = z_steps(q)
        up = jnp.where(z % 2 == 0, NZ - m, m)
        return at(x, (y - y_steps(n) + NY) % NY, (z + up) % NZ, core)

    pair_z = zh * 2 + 1 - zl
    pair, twin = at(x, y, pair_z, core), at(x, y, z, 1 - core)
    barrier = pltpu.get_barrier_semaphore()
    for q, n in FARTHEST:
        pl.semaphore_signal(barrier, inc=1, device_id=source(q, n), device_id_type=MESH)
    nearby = [along_x(-1), along_x(1), pair, twin]
    for peer in nearby:
        pl.semaphore_signal(barrier, inc=1, device_id=peer, device_id_type=MESH)

    for load in loads[:2]:
        load.wait()
    cid = cid_ref[...]
    residue = cid & (CLASSES - 1)
    dy = ((residue >> 2) - y) & (NY - 1)
    dz = (z - 2 * (residue & 3)) & (NZ - 1)
    member = jnp.where((dz == 0) | (dz > 4), (NZ - dz) & (NZ - 1), dz - 1)
    quarter = (4 - member) & 3
    place = jnp.where(dy <= 4, jnp.maximum(2 * dy - 1, 0), 2 * (NY - dy))
    offset = quarter * PER + place
    key = (cid >> 5) * SPAN + idx_ref[...] + 1
    offset_col = column_of(offset, ROWS)
    key_col = column_of(key, ROWS)
    first = lax.broadcasted_iota(jnp.int32, (ROWS, ROWS), 0)
    second = lax.broadcasted_iota(jnp.int32, (ROWS, ROWS), 1)
    equal = offset_col == offset
    rank = jnp.sum((equal & (first < second)).astype(jnp.int32), axis=0, keepdims=True)
    rank_col = jnp.sum((equal & (second < first)).astype(jnp.int32), axis=1, keepdims=True)
    lane = lax.broadcasted_iota(jnp.int32, (ROWS, 128), 1)
    digits = jnp.zeros((ROWS, 128), jnp.int32)
    for d, shift in enumerate((14, 7, 0)):
        digits = jnp.where(lane == SLOT * d + rank_col, (key_col >> shift) & 127, digits)
    digits = digits.astype(jnp.float32).astype(jnp.bfloat16)

    loads[2].wait()
    wide = emb_ref[...].astype(jnp.float32)
    inverse = lax.rsqrt(jnp.sum(wide * wide, axis=1, keepdims=True) + 1e-06)
    unit[...] = (wide * inverse).astype(jnp.bfloat16)
    for q in range(NQ):
        base = q * PER * SLOT
        slot = lax.broadcasted_iota(jnp.int32, (PER * SLOT, ROWS), 0) + base
        pick = to_bf16(slot == offset * SLOT + rank)
        pick_key = to_bf16(slot == offset * SLOT + CAP)
        rows = jnp.dot(pick, unit[...], preferred_element_type=jnp.float32)
        extra = jnp.dot(pick_key, digits, preferred_element_type=jnp.float32)
        send[base : base + PER * SLOT, :] = rows.astype(jnp.bfloat16)
        send[base : base + PER * SLOT, 0:128] = (rows[:, 0:128] + extra).astype(jnp.bfloat16)
    recv[0, 0:SLOT, :] = send[0:SLOT, :]
    best_k[...] = jnp.full(best_k.shape, -1.0, jnp.float32)
    best_q[...] = jnp.full(best_q.shape, -1.0, jnp.float32)
    for q in range(NQ):
        for s in range(2):
            for base in (CHUNK, 128 + CHUNK):
                query[q, s, base : base + 128 - CHUNK, :] = jnp.zeros(
                    (128 - CHUNK, DIM), jnp.bfloat16
                )

    pl.semaphore_wait(barrier, CLASSES - 1 + len(nearby))

    for q in range(NQ):
        for n in range(PER):
            if q or n:
                pltpu.make_async_remote_copy(
                    src_ref=send.at[pl.ds((q * PER + n) * SLOT, SLOT)],
                    dst_ref=recv.at[q, pl.ds(n * SLOT, SLOT)],
                    send_sem=a2a_send,
                    recv_sem=a2a_recv.at[q, n // 4],
                    device_id=home(q, n),
                    device_id_type=MESH,
                ).start()

    def part_of(q, j, h):
        start, size = (FIRST, CHUNK - FIRST) if h else (0, FIRST)
        if j < 2:
            return held.at[pl.ds(q * HELD + j * CHUNK + start, size)]
        return query.at[q, (j - 2) // 2, pl.ds((j - 2) % 2 * 128 + start, size)]

    copies = {}

    def pass_on(q, j, h, peer, to):
        copy = pltpu.make_async_remote_copy(
            src_ref=part_of(q, j, h), dst_ref=part_of(q, to, h),
            send_sem=y_send.at[q, to, h], recv_sem=y_recv.at[q, to, h],
            device_id=peer, device_id_type=MESH,
        )
        copy.start()
        copies[q, to, h] = copy
        if h:
            names = pltpu.make_async_remote_copy(
                src_ref=keys.at[q, j], dst_ref=keys.at[q, to],
                send_sem=k_send.at[q, to], recv_sem=k_recv.at[q, to],
                device_id=peer, device_id_type=MESH,
            )
            names.start()
            copies[q, to, 2] = names

    def arrived(q, j, h):
        copies[q, j, h].wait_recv()
        if h:
            copies[q, j, 2].wait_recv()

    def squeezer(start, size, below, width, nth=None):
        row = lax.broadcasted_iota(jnp.int32, (size, width), 0) + start
        col = lax.broadcasted_iota(jnp.int32, (size, width), 1) + below
        return to_bf16(col == row // CAP * SLOT + (row % CAP if nth is None else nth))

    squeeze = (
        squeezer(0, FIRST, 0, 4 * SLOT),
        squeezer(FIRST, CHUNK - FIRST, FIRST, PER * SLOT - FIRST),
    )
    key_rows = squeezer(0, CHUNK, 0, PER * SLOT, CAP)
    slot_col = lax.broadcasted_iota(jnp.int32, (CHUNK, PER * SLOT), 1)
    nth = lax.broadcasted_iota(jnp.int32, (CHUNK, PER * SLOT), 0) % CAP
    own_digit = (slot_col < 3 * SLOT) & (slot_col % SLOT == nth)
    digit_sum = to_bf16(
        lax.broadcasted_iota(jnp.int32, (8, 128), 1) // SLOT
        == lax.broadcasted_iota(jnp.int32, (8, 128), 0)
    )

    def own(q, h):
        skip = SLOT if q == 0 and h == 0 else 0
        landed = recv.at[q, pl.ds(h * 4 * SLOT + skip, 4 * SLOT - skip)]
        pltpu.make_async_copy(landed, landed, a2a_recv.at[q, h]).wait()
        base = q * HELD + CHUNK
        if h == 0:
            held[base : base + FIRST, :] = jnp.dot(
                squeeze[0], recv[q, 0 : 4 * SLOT, :], preferred_element_type=jnp.float32
            ).astype(jnp.bfloat16)
        else:
            held[base + FIRST : base + CHUNK, :] = jnp.dot(
                squeeze[1], recv[q, FIRST:, :], preferred_element_type=jnp.float32
            ).astype(jnp.bfloat16)
            spread = jnp.dot(key_rows, recv[q, :, 0:128], preferred_element_type=jnp.float32)
            spread = jnp.where(own_digit, spread, 0.0).astype(jnp.bfloat16)
            sums = contract_lanes(digit_sum, spread)
            value = sums[0:1] * 16384.0 + sums[1:2] * 128.0 + sums[2:3]
            keys[q, 1] = jnp.concatenate(
                [value, jnp.zeros((1, 128 - CHUNK), jnp.float32)], axis=1
            )
        pass_on(q, 1, h, along_x(-1), 2)
        pass_on(q, 1, h, along_x(1), 0)

    def own_copy(q, h):
        start, size = (FIRST, CHUNK - FIRST) if h else (0, FIRST)
        return pltpu.make_async_copy(
            part_of(q, 2, h),
            held.at[pl.ds(q * HELD + 2 * CHUNK + start, size)],
            own_sem.at[q, h],
        )

    def cross(q, h):
        arrived(q, 2, h)
        pass_on(q, 2, h, pair, 4)
        pass_on(q, 2, h, twin, 3)
        own_copy(q, h).start()

    def share(q, h):
        arrived(q, 4, h)
        pass_on(q, 4, h, twin, 5)

    def cluster_of(value):
        return jnp.floor((value - 1.0) * (1.0 / SPAN))

    def near(q):
        for h in range(2):
            arrived(q, 0, h)
            own_copy(q, h).wait()
        for j in range(3):
            column = jnp.broadcast_to(column_of(keys[q, j], CHUNK), (CHUNK, 128))
            base = q * HELD + j * CHUNK
            key_cols[base : base + CHUNK, :] = column
            clu_cols[base : base + CHUNK, :] = cluster_of(column)
        for h in range(2):
            arrived(q, 3, h)

    def far(q):
        for h in range(2):
            arrived(q, 5, h)

    def score(qk, qq, s):
        base = pl.multiple_of(qk * HELD, 16)
        scores[...] = contract_lanes(held[pl.ds(base, HELD), :], query[qq, s])
        key_row = [keys[qq, 2 + 2 * s + i] for i in range(2)]
        clu_row = [cluster_of(row) for row in key_row]
        tops = [best_q[qq, s, :, i * 128 : (i + 1) * 128] for i in range(2)]
        for g in range(HELD // 8):
            at_rows = pl.ds(pl.multiple_of(base + g * 8, 8), 8)
            key_here = key_cols[at_rows, :]
            clu_here = clu_cols[at_rows, :]
            top = best_k[at_rows, :]
            for i in range(2):
                value = scores[g * 8 : g * 8 + 8, i * 128 : (i + 1) * 128]
                value = jnp.where(clu_here == clu_row[i], value, -1.0)
                top = jnp.maximum(top, jnp.where(key_row[i] < key_here, value, -1.0))
                if CHUNK <= g * 8 < 2 * CHUNK:
                    tops[i] = jnp.maximum(tops[i], jnp.where(key_here < key_row[i], value, -1.0))
            best_k[at_rows, :] = top
        for i in range(2):
            best_q[qq, s, :, i * 128 : (i + 1) * 128] = tops[i]

    def score_all(count, pick):
        def step(t, carry):
            score(*pick(t))
            return carry

        lax.fori_loop(0, count, step, 0)

    def both_ways(q):
        def pick(t):
            k, s = t // 2, t % 2
            return jnp.where(k <= q, q, k - q - 1), jnp.where(k <= q, k, q), s

        return pick

    own(0, 0)
    own(0, 1)
    cross(0, 0)
    own(1, 0)
    cross(0, 1)
    own(1, 1)
    share(0, 0)
    own(2, 0)
    cross(1, 0)
    share(0, 1)
    cross(1, 1)
    own(2, 1)
    near(0)
    own(3, 0)
    cross(2, 0)
    share(1, 0)
    far(0)
    score_all(2, both_ways(0))
    own(3, 1)
    cross(2, 1)
    share(1, 1)
    near(1)
    far(1)
    share(2, 0)
    cross(3, 0)
    score_all(6, both_ways(1))
    cross(3, 1)
    share(2, 1)
    near(2)
    far(2)
    score_all(10, both_ways(2))
    share(3, 0)
    near(3)
    score_all(10, lambda t: (
        jnp.where(t < 6, 3, t - 6), jnp.where(t < 6, t // 2, 3), jnp.where(t < 6, t % 2, 0)
    ))
    share(3, 1)
    far(3)
    score_all(4, lambda t: (t, 3, 1))

    square = eye(CHUNK, 128)

    def over_query(q, j):
        base = q * HELD + j * CHUNK
        column = jnp.max(best_k[base : base + CHUNK, :], axis=1, keepdims=True)
        column = jnp.broadcast_to(column, (CHUNK, 128))
        return jnp.max(jnp.where(square, column, -1.0), axis=0, keepdims=True)

    for q in range(NQ):
        for u in range(4):
            lanes = slice(u % 2 * 128, u % 2 * 128 + 128)
            row = jnp.max(best_q[q, u // 2, :, lanes], axis=0, keepdims=True)
            if u == 0:
                row = jnp.maximum(row, over_query(q, 2))
            part_out[u, q : q + 1, :] = row
        part_out[4, q : q + 1, :] = over_query(q, 0)
    parts = []
    ahead = (x + 1) % NX
    for u, peer in enumerate((
        at(ahead, y, z, core), at(ahead, y, z, 1 - core),
        at(ahead, y, pair_z, core), at(ahead, y, pair_z, 1 - core), along_x(-1),
    )):
        part_out[u, NQ:8, :] = jnp.full((8 - NQ, 128), -1.0, jnp.float32)
        copy = pltpu.make_async_remote_copy(
            src_ref=part_out.at[u], dst_ref=part_in.at[u],
            send_sem=p_send.at[u], recv_sem=p_recv.at[u],
            device_id=peer, device_id_type=MESH,
        )
        copy.start()
        parts.append(copy)
    best = [over_query(q, 1) for q in range(NQ)]
    for u, copy in enumerate(parts):
        copy.wait_recv()
        best = [jnp.maximum(best[q], part_in[u, q : q + 1, :]) for q in range(NQ)]
    for q in range(NQ):
        final[q] = best[q]
    back[0] = best[0]

    for q, n in FARTHEST:
        pltpu.make_async_remote_copy(
            src_ref=final.at[q],
            dst_ref=back.at[q * PER + n],
            send_sem=b_send,
            recv_sem=b_recv,
            device_id=source(q, n),
            device_id_type=MESH,
        ).start()

    inbound = back.at[pl.ds(1, CLASSES - 1)]
    pltpu.make_async_copy(inbound, inbound, b_recv).wait()
    lane_row = lax.broadcasted_iota(jnp.int32, (1, 128), 1)
    hit = lax.broadcasted_iota(jnp.int32, (128, ROWS), 0) == place * CAP + rank
    result = jnp.zeros((1, ROWS), jnp.float32)
    for q in range(NQ):
        mine = jnp.zeros((1, 128), jnp.float32)
        for n in range(PER):
            mine = jnp.where(lane_row // CAP == n, back[q * PER + n], mine)
        column = jnp.broadcast_to(column_of(mine, 128), (128, ROWS))
        chosen = jnp.sum(jnp.where(hit, column, 0.0), axis=0, keepdims=True)
        result = jnp.where(quarter == q, chosen, result)
    out_ref[...] = result

    gone = send.at[pl.ds(SLOT, (CLASSES - 1) * SLOT)]
    pltpu.make_async_copy(gone, gone, a2a_send).wait()
    for copy in copies.values():
        copy.wait_send()
    for copy in parts:
        copy.wait_send()
    pltpu.make_async_copy(inbound, inbound, b_send).wait()


def per_device(embeddings, cluster_id, row_index):
    result = pl.pallas_call(
        kernel,
        out_shape=jax.ShapeDtypeStruct((1, ROWS), jnp.float32),
        in_specs=[pl.BlockSpec(memory_space=pl.ANY)] * 3,
        out_specs=pl.BlockSpec(memory_space=pltpu.VMEM),
        scratch_shapes=[
            pltpu.VMEM((ROWS, DIM), jnp.bfloat16),
            pltpu.VMEM((1, ROWS), jnp.int32),
            pltpu.VMEM((1, ROWS), jnp.int32),
            pltpu.VMEM((ROWS, DIM), jnp.bfloat16),
            pltpu.VMEM((CLASSES * SLOT, DIM), jnp.bfloat16),
            pltpu.VMEM((NQ, PER * SLOT, DIM), jnp.bfloat16),
            pltpu.VMEM((NQ * HELD, DIM), jnp.bfloat16),
            pltpu.VMEM((NQ, 2, 256, DIM), jnp.bfloat16),
            pltpu.VMEM((NQ, 6, 1, 128), jnp.float32),
            pltpu.VMEM((NQ * HELD, 128), jnp.float32),
            pltpu.VMEM((NQ * HELD, 128), jnp.float32),
            pltpu.VMEM((HELD, 256), jnp.float32),
            pltpu.VMEM((NQ * HELD, 128), jnp.float32),
            pltpu.VMEM((NQ, 2, 8, 256), jnp.float32),
            pltpu.VMEM((5, 8, 128), jnp.float32),
            pltpu.VMEM((5, 8, 128), jnp.float32),
            pltpu.VMEM((NQ, 1, 128), jnp.float32),
            pltpu.VMEM((CLASSES, 1, 128), jnp.float32),
            pltpu.SemaphoreType.DMA((3,)),
            pltpu.SemaphoreType.DMA((NQ, 2)),
            pltpu.SemaphoreType.DMA,
            pltpu.SemaphoreType.DMA((NQ, 2)),
            pltpu.SemaphoreType.DMA((NQ, 6, 2)),
            pltpu.SemaphoreType.DMA((NQ, 6, 2)),
            pltpu.SemaphoreType.DMA((NQ, 6)),
            pltpu.SemaphoreType.DMA((NQ, 6)),
            pltpu.SemaphoreType.DMA((5,)),
            pltpu.SemaphoreType.DMA((5,)),
            pltpu.SemaphoreType.DMA,
            pltpu.SemaphoreType.DMA,
        ],
        compiler_params=pltpu.CompilerParams(
            collective_id=0, has_side_effects=True, vmem_limit_bytes=62 * 1024 * 1024
        ),
    )(embeddings, cluster_id.reshape(1, ROWS), row_index.reshape(1, ROWS))
    return result.reshape(ROWS)


def solution(mesh):
    placed = (P(("owner", "panel"), None), P(("owner", "panel")), P(("owner", "panel")))
    return jax.shard_map(
        per_device, mesh=mesh, in_specs=placed, out_specs=P(("owner", "panel")), check_vma=False
    )
```

time: 80.3 us -> 78 us (0.971)
  Pallas kernels: 77.8 us -> 76.6 us
  local copies, waits for them, and re-layouts: 2.28 us -> 1.22 us
    pallas_call x1, Pallas kernels: 77.8 us -> 76.6 us  [per_device(): pl.pallas_call(kernel, out_shape=jax.ShapeDtypeStruct((1, ROWS), jnp.floa...]
    unnamed x7 -> x3, local copies, waits for them, and re-layouts: 2.28 us -> 1.22 us
where the time goes in v3:
time: 78 us; the launch traced here: 77.8 us
  Pallas kernels  76.6 us (98%)
  local copies, waits for them, and re-layouts  1.22 us (2%)
    pallas_call x1, Pallas kernels, per_device(): pl.pallas_call(kernel, out_shape=jax.ShapeDtypeStruct((1, ROWS), jnp.floa...  76.6 us

profile of v3, /device:TPU:1, one launch (start us, length us, event | category | flops | bytes accessed | tf_op | source)
XLA Modules:
  0.0 77.8 jit_solution(1155412717975546782)
XLA Ops:
  0.0 76.6 %shard_map.37 = f32[1,224]{1,0:T(1,128)} custom-call(bf16[224,1024]{1,0:T(8,128)(2,1)} %emb_hbm.1, s32[1,224]{1,0:T(1,128)} %bitcast.4, s32[1,224]{1,0:T(1,128)} %bitcast.5), custom_call_target="tpu_custom_call" | custom-call | tf_op jit(solution)/shard_map/pallas_call | solution.py:422
  76.6 0.0 copy-start
  76.6 0.7 copy-done
  77.3 0.6 copy.5
Async XLA Ops:
  76.6 0.7 copy-start

commit v4 on v3

--- a/solution.py
+++ b/solution.py
@@ -131,28 +131,17 @@
     wide = emb_ref[...].astype(jnp.float32)
     inverse = lax.rsqrt(jnp.sum(wide * wide, axis=1, keepdims=True) + 1e-06)
     unit[...] = (wide * inverse).astype(jnp.bfloat16)
-    for q in range(NQ):
+    def slotted(q):
         base = q * PER * SLOT
         slot = lax.broadcasted_iota(jnp.int32, (PER * SLOT, ROWS), 0) + base
         pick = to_bf16(slot == offset * SLOT + rank)
         pick_key = to_bf16(slot == offset * SLOT + CAP)
         rows = jnp.dot(pick, unit[...], preferred_element_type=jnp.float32)
         extra = jnp.dot(pick_key, digits, preferred_element_type=jnp.float32)
-        send[base : base + PER * SLOT, :] = rows.astype(jnp.bfloat16)
+        send[base : base + PER * SLOT, 128:] = rows[:, 128:].astype(jnp.bfloat16)
         send[base : base + PER * SLOT, 0:128] = (rows[:, 0:128] + extra).astype(jnp.bfloat16)
-    recv[0, 0:SLOT, :] = send[0:SLOT, :]
-    best_k[...] = jnp.full(best_k.shape, -1.0, jnp.float32)
-    best_q[...] = jnp.full(best_q.shape, -1.0, jnp.float32)
-    for q in range(NQ):
-        for s in range(2):
-            for base in (CHUNK, 128 + CHUNK):
-                query[q, s, base : base + 128 - CHUNK, :] = jnp.zeros(
-                    (128 - CHUNK, DIM), jnp.bfloat16
-                )
-
-    pl.semaphore_wait(barrier, CLASSES - 1 + len(nearby))
-
-    for q in range(NQ):
+
+    def give(q):
         for n in range(PER):
             if q or n:
                 pltpu.make_async_remote_copy(
@@ -163,6 +152,22 @@
                     device_id=home(q, n),
                     device_id_type=MESH,
                 ).start()
+
+    slotted(0)
+    pl.semaphore_wait(barrier, CLASSES - 1 + len(nearby))
+    for q in range(NQ):
+        if q:
+            slotted(q)
+        give(q)
+    recv[0, 0:SLOT, :] = send[0:SLOT, :]
+    best_k[...] = jnp.full(best_k.shape, -1.0, jnp.float32)
+    best_q[...] = jnp.full(best_q.shape, -1.0, jnp.float32)
+    for q in range(NQ):
+        for s in range(2):
+            for base in (CHUNK, 128 + CHUNK):
+                query[q, s, base : base + 128 - CHUNK, :] = jnp.zeros(
+                    (128 - CHUNK, DIM), jnp.bfloat16
+                )
 
     def part_of(q, j, h):
         start, size = (FIRST, CHUNK - FIRST) if h else (0, FIRST)
@@ -272,14 +277,47 @@
         for h in range(2):
             arrived(q, 5, h)
 
-    def score(qk, qq, s):
-        base = pl.multiple_of(qk * HELD, 16)
-        scores[...] = contract_lanes(held[pl.ds(base, HELD), :], query[qq, s])
+    def score(first, count, qq, s):
+        rows = count * HELD
+        scores[0:rows, :] = contract_lanes(
+            held[first * HELD : first * HELD + rows, :], query[qq, s]
+        )
+        key_row = [keys[qq, 2 + 2 * s + i] for i in range(2)]
+        clu_row = [cluster_of(row) for row in key_row]
+
+        def one_chunk(k, tops):
+            tops = list(tops)
+            base = pl.multiple_of((first + k) * HELD, 8)
+            for g in range(HELD // 8):
+                at_rows = pl.ds(base + g * 8, 8)
+                from_rows = pl.ds(pl.multiple_of(k * HELD, 8) + g * 8, 8)
+                key_here = key_cols[at_rows, :]
+                clu_here = clu_cols[at_rows, :]
+                top = best_k[at_rows, :]
+                for i in range(2):
+                    value = scores[from_rows, i * 128 : (i + 1) * 128]
+                    value = jnp.where(clu_here == clu_row[i], value, -1.0)
+                    top = jnp.maximum(top, jnp.where(key_row[i] < key_here, value, -1.0))
+                    if CHUNK <= g * 8 < 2 * CHUNK:
+                        tops[i] = jnp.maximum(
+                            tops[i], jnp.where(key_here < key_row[i], value, -1.0)
+                        )
+                best_k[at_rows, :] = top
+            return tuple(tops)
+
+        tops = tuple(best_q[qq, s, :, i * 128 : (i + 1) * 128] for i in range(2))
+        tops = lax.fori_loop(0, count, one_chunk, tops)
+        for i in range(2):
+            best_q[qq, s, :, i * 128 : (i + 1) * 128] = tops[i]
+
+    def score_one(k, qq, s):
+        base = pl.multiple_of(k * HELD, 16)
+        scores[0:HELD, :] = contract_lanes(held[pl.ds(base, HELD), :], query[qq, s])
         key_row = [keys[qq, 2 + 2 * s + i] for i in range(2)]
         clu_row = [cluster_of(row) for row in key_row]
         tops = [best_q[qq, s, :, i * 128 : (i + 1) * 128] for i in range(2)]
         for g in range(HELD // 8):
-            at_rows = pl.ds(pl.multiple_of(base + g * 8, 8), 8)
+            at_rows = pl.ds(base + g * 8, 8)
             key_here = key_cols[at_rows, :]
             clu_here = clu_cols[at_rows, :]
             top = best_k[at_rows, :]
@@ -293,19 +331,12 @@
         for i in range(2):
             best_q[qq, s, :, i * 128 : (i + 1) * 128] = tops[i]
 
-    def score_all(count, pick):
+    def score_halves(first, count, start, stop):
         def step(t, carry):
-            score(*pick(t))
+            score(first, count, t // 2, t % 2)
             return carry
 
-        lax.fori_loop(0, count, step, 0)
-
-    def both_ways(q):
-        def pick(t):
-            k, s = t // 2, t % 2
-            return jnp.where(k <= q, q, k - q - 1), jnp.where(k <= q, k, q), s
-
-        return pick
+        lax.fori_loop(start, stop, step, 0)
 
     own(0, 0)
     own(0, 1)
@@ -320,32 +351,35 @@
     cross(1, 1)
     own(2, 1)
     near(0)
+    far(0)
     own(3, 0)
     cross(2, 0)
     share(1, 0)
-    far(0)
-    score_all(2, both_ways(0))
     own(3, 1)
     cross(2, 1)
     share(1, 1)
     near(1)
-    far(1)
+    near(2)
+    score_halves(0, 3, 0, 2)
     share(2, 0)
     cross(3, 0)
-    score_all(6, both_ways(1))
+    far(1)
+    share(2, 1)
     cross(3, 1)
-    share(2, 1)
-    near(2)
+    score_halves(0, 3, 2, 4)
+    near(3)
+    score_halves(3, 1, 0, 4)
     far(2)
-    score_all(10, both_ways(2))
     share(3, 0)
-    near(3)
-    score_all(10, lambda t: (
-        jnp.where(t < 6, 3, t - 6), jnp.where(t < 6, t // 2, 3), jnp.where(t < 6, t % 2, 0)
-    ))
+    score_halves(0, 4, 4, 6)
+    score(0, 4, 3, 0)
     share(3, 1)
     far(3)
-    score_all(4, lambda t: (t, 3, 1))
+    def last(k, carry):
+        score_one(k, 3, 1)
+        return carry
+
+    lax.fori_loop(0, NQ, last, 0)
 
     square = eye(CHUNK, 128)
 
@@ -436,7 +470,7 @@
             pltpu.VMEM((NQ, 6, 1, 128), jnp.float32),
             pltpu.VMEM((NQ * HELD, 128), jnp.float32),
             pltpu.VMEM((NQ * HELD, 128), jnp.float32),
-            pltpu.VMEM((HELD, 256), jnp.float32),
+            pltpu.VMEM((NQ * HELD, 256), jnp.float32),
             pltpu.VMEM((NQ * HELD, 128), jnp.float32),
             pltpu.VMEM((NQ, 2, 8, 256), jnp.float32),
             pltpu.VMEM((5, 8, 128), jnp.float32),

time: 78 us -> 74.9 us (0.960)
  Pallas kernels: 76.6 us -> 73.6 us
    pallas_call x1, Pallas kernels: 76.6 us -> 73.6 us  [per_device(): pl.pallas_call(kernel, out_shape=jax.ShapeDtypeStruct((1, ROWS), jnp.floa...]
where the time goes in v4:
time: 74.9 us; the launch traced here: 74.8 us
  Pallas kernels  73.6 us (98%)
  local copies, waits for them, and re-layouts  1.22 us (2%)
    pallas_call x1, Pallas kernels, per_device(): pl.pallas_call(kernel, out_shape=jax.ShapeDtypeStruct((1, ROWS), jnp.floa...  73.6 us

profile of v4, /device:TPU:1, one launch (start us, length us, event | category | flops | bytes accessed | tf_op | source)
XLA Modules:
  0.0 74.8 jit_solution(520757860955306273)
XLA Ops:
  0.0 73.6 %shard_map.37 = f32[1,224]{1,0:T(1,128)} custom-call(bf16[224,1024]{1,0:T(8,128)(2,1)} %emb_hbm.1, s32[1,224]{1,0:T(1,128)} %bitcast.4, s32[1,224]{1,0:T(1,128)} %bitcast.5), custom_call_target="tpu_custom_call" | custom-call | tf_op jit(solution)/shard_map/pallas_call | solution.py:456
  73.6 0.0 copy-start
  73.6 0.7 copy-done
  74.2 0.6 copy.5
Async XLA Ops:
  73.6 0.7 copy-start

commit v5 on v4

--- a/solution.py
+++ b/solution.py
@@ -51,6 +51,9 @@
 
 
 FIRST = 48
+TILES = 7
+PACKED = TILES * 128
+SPARE = PER * (SLOT - CAP)
 FARTHEST = sorted(
     ((q, n) for q in range(NQ) for n in range(PER) if q or n),
     key=lambda slot: -(z_steps(slot[0]) + (slot[1] + 1) // 2),
@@ -59,9 +62,9 @@
 
 def kernel(
     emb_hbm, cid_hbm, idx_hbm, out_ref,
-    emb_ref, cid_ref, idx_ref, unit, send, recv, held, query, keys, key_cols, clu_cols, scores,
+    emb_ref, cid_ref, idx_ref, slots, unit, send, recv, key_out, key_in, held, query, keys, key_cols, clu_cols, scores,
     best_k, best_q, part_out, part_in, final, back,
-    in_sem, own_sem, a2a_send, a2a_recv, y_send, y_recv, k_send, k_recv, p_send, p_recv, b_send, b_recv,
+    in_sem, own_sem, a2a_send, a2a_recv, n_send, n_recv, y_send, y_recv, k_send, k_recv, p_send, p_recv, b_send, b_recv,
 ):
     owner = lax.axis_index("owner")
     panel = lax.axis_index("panel")
@@ -121,25 +124,33 @@
     equal = offset_col == offset
     rank = jnp.sum((equal & (first < second)).astype(jnp.int32), axis=0, keepdims=True)
     rank_col = jnp.sum((equal & (second < first)).astype(jnp.int32), axis=1, keepdims=True)
-    lane = lax.broadcasted_iota(jnp.int32, (ROWS, 128), 1)
-    digits = jnp.zeros((ROWS, 128), jnp.int32)
-    for d, shift in enumerate((14, 7, 0)):
-        digits = jnp.where(lane == SLOT * d + rank_col, (key_col >> shift) & 127, digits)
-    digits = digits.astype(jnp.float32).astype(jnp.bfloat16)
+    slots[...] = jnp.zeros(slots.shape, jnp.int32)
+    slots[:, 0:ROWS] = offset * SLOT + rank
 
     loads[2].wait()
     wide = emb_ref[...].astype(jnp.float32)
     inverse = lax.rsqrt(jnp.sum(wide * wide, axis=1, keepdims=True) + 1e-06)
-    unit[...] = (wide * inverse).astype(jnp.bfloat16)
+    unit[0:ROWS, :] = (wide * inverse).astype(jnp.bfloat16)
+    depth = ROWS + SPARE
+    lane = lax.broadcasted_iota(jnp.int32, (1, depth), 1)
+    extra = lane - ROWS
+    extra = (extra >> 1) * SLOT + CAP + (extra & 1)
+    row = lax.broadcasted_iota(jnp.int32, (TILES * SPARE, ROWS), 0)
+    tail_slot = ((row & (SPARE - 1)) >> 1) * SLOT + (row >> 4) + (row & 1) * TILES
+    plain = lax.broadcasted_iota(jnp.int32, (PER * SLOT, depth), 0)
+
     def slotted(q):
         base = q * PER * SLOT
-        slot = lax.broadcasted_iota(jnp.int32, (PER * SLOT, ROWS), 0) + base
-        pick = to_bf16(slot == offset * SLOT + rank)
-        pick_key = to_bf16(slot == offset * SLOT + CAP)
-        rows = jnp.dot(pick, unit[...], preferred_element_type=jnp.float32)
-        extra = jnp.dot(pick_key, digits, preferred_element_type=jnp.float32)
-        send[base : base + PER * SLOT, 128:] = rows[:, 128:].astype(jnp.bfloat16)
-        send[base : base + PER * SLOT, 0:128] = (rows[:, 0:128] + extra).astype(jnp.bfloat16)
+        tails = jnp.dot(
+            to_bf16(tail_slot == slots[:, 0:ROWS] - base),
+            unit[0:ROWS, PACKED:], preferred_element_type=jnp.float32,
+        ).astype(jnp.bfloat16)
+        for t in range(TILES):
+            unit[ROWS:depth, t * 128 : t * 128 + 128] = tails[t * SPARE : (t + 1) * SPARE]
+        pick = plain == jnp.where(lane < ROWS, slots[:, 0:depth] - base, extra)
+        send[base : base + PER * SLOT, :] = jnp.dot(
+            to_bf16(pick), unit[:, 0:PACKED], preferred_element_type=jnp.float32
+        ).astype(jnp.bfloat16)
 
     def give(q):
         for n in range(PER):
@@ -155,19 +166,43 @@
 
     slotted(0)
     pl.semaphore_wait(barrier, CLASSES - 1 + len(nearby))
-    for q in range(NQ):
-        if q:
-            slotted(q)
-        give(q)
-    recv[0, 0:SLOT, :] = send[0:SLOT, :]
-    best_k[...] = jnp.full(best_k.shape, -1.0, jnp.float32)
-    best_q[...] = jnp.full(best_q.shape, -1.0, jnp.float32)
-    for q in range(NQ):
-        for s in range(2):
-            for base in (CHUNK, 128 + CHUNK):
-                query[q, s, base : base + 128 - CHUNK, :] = jnp.zeros(
-                    (128 - CHUNK, DIM), jnp.bfloat16
-                )
+    def clear():
+        best_k[...] = jnp.full(best_k.shape, -1.0, jnp.float32)
+        best_q[...] = jnp.full(best_q.shape, -1.0, jnp.float32)
+        for q in range(NQ):
+            for s in range(2):
+                for base in (CHUNK, 128 + CHUNK):
+                    query[q, s, base : base + 128 - CHUNK, :] = jnp.zeros(
+                        (128 - CHUNK, DIM), jnp.bfloat16
+                    )
+
+    def fill_keys():
+        here = lax.broadcasted_iota(jnp.int32, (ROWS, 128), 1) == (
+            (offset_col & (PER - 1)) * CAP + rank_col
+        )
+        ours = to_bf16(lax.broadcasted_iota(jnp.int32, (CLASSES, ROWS), 0) == offset)
+        digits = [
+            jnp.where(here, (key_col >> shift) & 127, 0).astype(jnp.float32).astype(jnp.bfloat16)
+            for shift in (14, 7, 0)
+        ]
+        table = jnp.dot(
+            ours, jnp.concatenate(digits, axis=1), preferred_element_type=jnp.float32
+        )
+        table = table[:, 0:128] * 16384.0 + table[:, 128:256] * 128.0 + table[:, 256:384]
+        for k in range(CLASSES):
+            key_out[k] = table[k : k + 1, :]
+        key_in[0] = key_out[0]
+
+    def give_keys(part):
+        for q, n in FARTHEST[part * 8 : part * 8 + 8]:
+            pltpu.make_async_remote_copy(
+                src_ref=key_out.at[q * PER + n],
+                dst_ref=key_in.at[q * PER + n],
+                send_sem=n_send,
+                recv_sem=n_recv,
+                device_id=home(q, n),
+                device_id_type=MESH,
+            ).start()
 
     def part_of(q, j, h):
         start, size = (FIRST, CHUNK - FIRST) if h else (0, FIRST)
@@ -185,60 +220,82 @@
         )
         copy.start()
         copies[q, to, h] = copy
-        if h:
-            names = pltpu.make_async_remote_copy(
-                src_ref=keys.at[q, j], dst_ref=keys.at[q, to],
-                send_sem=k_send.at[q, to], recv_sem=k_recv.at[q, to],
-                device_id=peer, device_id_type=MESH,
-            )
-            names.start()
-            copies[q, to, 2] = names
+
+    def pass_keys(j, peer, to):
+        copy = pltpu.make_async_remote_copy(
+            src_ref=keys.at[j], dst_ref=keys.at[to],
+            send_sem=k_send.at[to], recv_sem=k_recv.at[to],
+            device_id=peer, device_id_type=MESH,
+        )
+        copy.start()
+        copies["keys", to] = copy
 
     def arrived(q, j, h):
         copies[q, j, h].wait_recv()
-        if h:
-            copies[q, j, 2].wait_recv()
 
     def squeezer(start, size, below, width, nth=None):
         row = lax.broadcasted_iota(jnp.int32, (size, width), 0) + start
         col = lax.broadcasted_iota(jnp.int32, (size, width), 1) + below
         return to_bf16(col == row // CAP * SLOT + (row % CAP if nth is None else nth))
 
-    squeeze = (
-        squeezer(0, FIRST, 0, 4 * SLOT),
-        squeezer(FIRST, CHUNK - FIRST, FIRST, PER * SLOT - FIRST),
-    )
-    key_rows = squeezer(0, CHUNK, 0, PER * SLOT, CAP)
-    slot_col = lax.broadcasted_iota(jnp.int32, (CHUNK, PER * SLOT), 1)
-    nth = lax.broadcasted_iota(jnp.int32, (CHUNK, PER * SLOT), 0) % CAP
-    own_digit = (slot_col < 3 * SLOT) & (slot_col % SLOT == nth)
-    digit_sum = to_bf16(
-        lax.broadcasted_iota(jnp.int32, (8, 128), 1) // SLOT
-        == lax.broadcasted_iota(jnp.int32, (8, 128), 0)
+    def unpacker(start, size, below, width):
+        row = lax.broadcasted_iota(jnp.int32, (size + SPARE, width), 0)
+        col = lax.broadcasted_iota(jnp.int32, (size + SPARE, width), 1) + below
+        spare = row - size
+        spare = (spare >> 1) * SLOT + CAP + (spare & 1)
+        row = row + start
+        main = col == jnp.where(row < start + size, row // CAP * SLOT + row % CAP, spare)
+        row = lax.broadcasted_iota(jnp.int32, (size, TILES * SPARE), 0) + start
+        col = lax.broadcasted_iota(jnp.int32, (size, TILES * SPARE), 1)
+        tail = (row // CAP == (col & (SPARE - 1)) >> 1) & (
+            row % CAP == (col >> 4) + (col & 1) * TILES
+        )
+        return below, width, to_bf16(main), to_bf16(tail)
+
+    unpack = (
+        unpacker(0, FIRST, 0, 4 * SLOT),
+        unpacker(FIRST, CHUNK - FIRST, FIRST, PER * SLOT - FIRST),
     )
 
     def own(q, h):
         skip = SLOT if q == 0 and h == 0 else 0
         landed = recv.at[q, pl.ds(h * 4 * SLOT + skip, 4 * SLOT - skip)]
         pltpu.make_async_copy(landed, landed, a2a_recv.at[q, h]).wait()
-        base = q * HELD + CHUNK
-        if h == 0:
-            held[base : base + FIRST, :] = jnp.dot(
-                squeeze[0], recv[q, 0 : 4 * SLOT, :], preferred_element_type=jnp.float32
-            ).astype(jnp.bfloat16)
-        else:
-            held[base + FIRST : base + CHUNK, :] = jnp.dot(
-                squeeze[1], recv[q, FIRST:, :], preferred_element_type=jnp.float32
-            ).astype(jnp.bfloat16)
-            spread = jnp.dot(key_rows, recv[q, :, 0:128], preferred_element_type=jnp.float32)
-            spread = jnp.where(own_digit, spread, 0.0).astype(jnp.bfloat16)
-            sums = contract_lanes(digit_sum, spread)
-            value = sums[0:1] * 16384.0 + sums[1:2] * 128.0 + sums[2:3]
-            keys[q, 1] = jnp.concatenate(
-                [value, jnp.zeros((1, 128 - CHUNK), jnp.float32)], axis=1
-            )
+        below, width, main, tail = unpack[h]
+        size = tail.shape[0]
+        base = q * HELD + CHUNK + h * FIRST
+        rows = jnp.dot(
+            main, recv[q, below : below + width, :], preferred_element_type=jnp.float32
+        ).astype(jnp.bfloat16)
+        held[base : base + size, 0:PACKED] = rows[0:size]
+        last = jnp.concatenate(
+            [rows[size:, t * 128 : t * 128 + 128] for t in range(TILES)], axis=0
+        )
+        held[base : base + size, PACKED:] = jnp.dot(
+            tail, last, preferred_element_type=jnp.float32
+        ).astype(jnp.bfloat16)
         pass_on(q, 1, h, along_x(-1), 2)
         pass_on(q, 1, h, along_x(1), 0)
+
+    def own_keys():
+        names = key_in.at[pl.ds(1, CLASSES - 1)]
+        pltpu.make_async_copy(names, names, n_recv).wait()
+        for q in range(NQ):
+            total = key_in[q * PER]
+            for n in range(1, PER):
+                total = total + key_in[q * PER + n]
+            keys[1, q] = total
+        pass_keys(1, along_x(-1), 2)
+        pass_keys(1, along_x(1), 0)
+
+    def cross_keys():
+        copies["keys", 2].wait_recv()
+        pass_keys(2, pair, 4)
+        pass_keys(2, twin, 3)
+
+    def share_keys():
+        copies["keys", 4].wait_recv()
+        pass_keys(4, twin, 5)
 
     def own_copy(q, h):
         start, size = (FIRST, CHUNK - FIRST) if h else (0, FIRST)
@@ -261,15 +318,20 @@
     def cluster_of(value):
         return jnp.floor((value - 1.0) * (1.0 / SPAN))
 
+    def all_keys():
+        for j in (0, 3, 5):
+            copies["keys", j].wait_recv()
+        for q in range(NQ):
+            for j in range(3):
+                column = jnp.broadcast_to(column_of(keys[j, q], CHUNK), (CHUNK, 128))
+                base = q * HELD + j * CHUNK
+                key_cols[base : base + CHUNK, :] = column
+                clu_cols[base : base + CHUNK, :] = cluster_of(column)
+
     def near(q):
         for h in range(2):
             arrived(q, 0, h)
             own_copy(q, h).wait()
-        for j in range(3):
-            column = jnp.broadcast_to(column_of(keys[q, j], CHUNK), (CHUNK, 128))
-            base = q * HELD + j * CHUNK
-            key_cols[base : base + CHUNK, :] = column
-            clu_cols[base : base + CHUNK, :] = cluster_of(column)
         for h in range(2):
             arrived(q, 3, h)
 
@@ -282,7 +344,7 @@
         scores[0:rows, :] = contract_lanes(
             held[first * HELD : first * HELD + rows, :], query[qq, s]
         )
-        key_row = [keys[qq, 2 + 2 * s + i] for i in range(2)]
+        key_row = [keys[2 + 2 * s + i, qq] for i in range(2)]
         clu_row = [cluster_of(row) for row in key_row]
 
         def one_chunk(k, tops):
@@ -310,13 +372,14 @@
         for i in range(2):
             best_q[qq, s, :, i * 128 : (i + 1) * 128] = tops[i]
 
-    def score_one(k, qq, s):
-        base = pl.multiple_of(k * HELD, 16)
-        scores[0:HELD, :] = contract_lanes(held[pl.ds(base, HELD), :], query[qq, s])
-        key_row = [keys[qq, 2 + 2 * s + i] for i in range(2)]
+    def score_rows(first, count, qq, s):
+        rows = count * HELD
+        base = pl.multiple_of(first * HELD, 16)
+        scores[0:rows, :] = contract_lanes(held[pl.ds(base, rows), :], query[qq, s])
+        key_row = [keys[2 + 2 * s + i, qq] for i in range(2)]
         clu_row = [cluster_of(row) for row in key_row]
         tops = [best_q[qq, s, :, i * 128 : (i + 1) * 128] for i in range(2)]
-        for g in range(HELD // 8):
+        for g in range(rows // 8):
             at_rows = pl.ds(base + g * 8, 8)
             key_here = key_cols[at_rows, :]
             clu_here = clu_cols[at_rows, :]
@@ -325,7 +388,7 @@
                 value = scores[g * 8 : g * 8 + 8, i * 128 : (i + 1) * 128]
                 value = jnp.where(clu_here == clu_row[i], value, -1.0)
                 top = jnp.maximum(top, jnp.where(key_row[i] < key_here, value, -1.0))
-                if CHUNK <= g * 8 < 2 * CHUNK:
+                if CHUNK <= g * 8 % HELD < 2 * CHUNK:
                     tops[i] = jnp.maximum(tops[i], jnp.where(key_here < key_row[i], value, -1.0))
             best_k[at_rows, :] = top
         for i in range(2):
@@ -338,25 +401,47 @@
 
         lax.fori_loop(start, stop, step, 0)
 
+    def score_list(times, pick):
+        def step(t, carry):
+            score_rows(*pick(t))
+            return carry
+
+        lax.fori_loop(0, times, step, 0)
+
+    give(0)
+    recv[0, 0:SLOT, :] = send[0:SLOT, :]
+    for q in range(1, NQ):
+        slotted(q)
+        give(q)
     own(0, 0)
     own(0, 1)
+    fill_keys()
+    give_keys(0)
     cross(0, 0)
+    give_keys(1)
     own(1, 0)
+    give_keys(2)
     cross(0, 1)
+    give_keys(3)
     own(1, 1)
+    clear()
     share(0, 0)
     own(2, 0)
     cross(1, 0)
+    own_keys()
     share(0, 1)
     cross(1, 1)
     own(2, 1)
+    cross_keys()
     near(0)
     far(0)
     own(3, 0)
     cross(2, 0)
+    share_keys()
     share(1, 0)
     own(3, 1)
     cross(2, 1)
+    all_keys()
     share(1, 1)
     near(1)
     near(2)
@@ -371,15 +456,15 @@
     score_halves(3, 1, 0, 4)
     far(2)
     share(3, 0)
-    score_halves(0, 4, 4, 6)
-    score(0, 4, 3, 0)
+    score_list(4, lambda t: (t % 2 * 2, 2, 2, t // 2))
     share(3, 1)
+    score_list(2, lambda t: (t * 2, 2, 3, 0))
     far(3)
     def last(k, carry):
-        score_one(k, 3, 1)
+        score_rows(2 * k, 2, 3, 1)
         return carry
 
-    lax.fori_loop(0, NQ, last, 0)
+    lax.fori_loop(0, NQ // 2, last, 0)
 
     square = eye(CHUNK, 128)
 
@@ -445,6 +530,8 @@
 
     gone = send.at[pl.ds(SLOT, (CLASSES - 1) * SLOT)]
     pltpu.make_async_copy(gone, gone, a2a_send).wait()
+    told = key_out.at[pl.ds(1, CLASSES - 1)]
+    pltpu.make_async_copy(told, told, n_send).wait()
     for copy in copies.values():
         copy.wait_send()
     for copy in parts:
@@ -462,12 +549,15 @@
             pltpu.VMEM((ROWS, DIM), jnp.bfloat16),
             pltpu.VMEM((1, ROWS), jnp.int32),
             pltpu.VMEM((1, ROWS), jnp.int32),
-            pltpu.VMEM((ROWS, DIM), jnp.bfloat16),
-            pltpu.VMEM((CLASSES * SLOT, DIM), jnp.bfloat16),
-            pltpu.VMEM((NQ, PER * SLOT, DIM), jnp.bfloat16),
+            pltpu.VMEM((1, 256), jnp.int32),
+            pltpu.VMEM((ROWS + SPARE, DIM), jnp.bfloat16),
+            pltpu.VMEM((CLASSES * SLOT, PACKED), jnp.bfloat16),
+            pltpu.VMEM((NQ, PER * SLOT, PACKED), jnp.bfloat16),
+            pltpu.VMEM((CLASSES, 1, 128), jnp.float32),
+            pltpu.VMEM((CLASSES, 1, 128), jnp.float32),
             pltpu.VMEM((NQ * HELD, DIM), jnp.bfloat16),
             pltpu.VMEM((NQ, 2, 256, DIM), jnp.bfloat16),
-            pltpu.VMEM((NQ, 6, 1, 128), jnp.float32),
+            pltpu.VMEM((6, NQ, 1, 128), jnp.float32),
             pltpu.VMEM((NQ * HELD, 128), jnp.float32),
             pltpu.VMEM((NQ * HELD, 128), jnp.float32),
             pltpu.VMEM((NQ * HELD, 256), jnp.float32),
@@ -481,10 +571,12 @@
             pltpu.SemaphoreType.DMA((NQ, 2)),
             pltpu.SemaphoreType.DMA,
             pltpu.SemaphoreType.DMA((NQ, 2)),
+            pltpu.SemaphoreType.DMA,
+            pltpu.SemaphoreType.DMA,
             pltpu.SemaphoreType.DMA((NQ, 6, 2)),
             pltpu.SemaphoreType.DMA((NQ, 6, 2)),
-            pltpu.SemaphoreType.DMA((NQ, 6)),
-            pltpu.SemaphoreType.DMA((NQ, 6)),
+            pltpu.SemaphoreType.DMA((6,)),
+            pltpu.SemaphoreType.DMA((6,)),
             pltpu.SemaphoreType.DMA((5,)),
             pltpu.SemaphoreType.DMA((5,)),
             pltpu.SemaphoreType.DMA,

time: 74.9 us -> 72.6 us (0.969)
  Pallas kernels: 73.6 us -> 71.2 us
    pallas_call x1, Pallas kernels: 73.6 us -> 71.2 us  [per_device(): pl.pallas_call(kernel, out_shape=jax.ShapeDtypeStruct((1, ROWS), jnp.floa...]
where the time goes in v5:
time: 72.6 us; the launch traced here: 72.4 us
  Pallas kernels  71.2 us (98%)
  local copies, waits for them, and re-layouts  1.22 us (2%)
    pallas_call x1, Pallas kernels, per_device(): pl.pallas_call(kernel, out_shape=jax.ShapeDtypeStruct((1, ROWS), jnp.floa...  71.2 us

profile of v5, /device:TPU:1, one launch (start us, length us, event | category | flops | bytes accessed | tf_op | source)
XLA Modules:
  0.0 72.4 jit_solution(12240182921445428911)
XLA Ops:
  0.0 71.2 %shard_map.37 = f32[1,224]{1,0:T(1,128)} custom-call(bf16[224,1024]{1,0:T(8,128)(2,1)} %emb_hbm.1, s32[1,224]{1,0:T(1,128)} %bitcast.4, s32[1,224]{1,0:T(1,128)} %bitcast.5), custom_call_target="tpu_custom_call" | custom-call | tf_op jit(solution)/shard_map/pallas_call | solution.py:543
  71.2 0.0 copy-start
  71.2 0.7 copy-done
  71.9 0.6 copy.5
Async XLA Ops:
  71.2 0.7 copy-start

commit v6 on v5

--- a/solution.py
+++ b/solution.py
@@ -58,6 +58,12 @@
     ((q, n) for q in range(NQ) for n in range(PER) if q or n),
     key=lambda slot: -(z_steps(slot[0]) + (slot[1] + 1) // 2),
 )
+
+
+def held_row(q, j):
+    if j == 1:
+        return q * CHUNK
+    return NQ * CHUNK + (NQ - 1 - q) * 2 * CHUNK + j // 2 * CHUNK
 
 
 def kernel(
@@ -207,7 +213,7 @@
     def part_of(q, j, h):
         start, size = (FIRST, CHUNK - FIRST) if h else (0, FIRST)
         if j < 2:
-            return held.at[pl.ds(q * HELD + j * CHUNK + start, size)]
+            return held.at[pl.ds(held_row(q, j) + start, size)]
         return query.at[q, (j - 2) // 2, pl.ds((j - 2) % 2 * 128 + start, size)]
 
     copies = {}
@@ -263,7 +269,7 @@
         pltpu.make_async_copy(landed, landed, a2a_recv.at[q, h]).wait()
         below, width, main, tail = unpack[h]
         size = tail.shape[0]
-        base = q * HELD + CHUNK + h * FIRST
+        base = held_row(q, 1) + h * FIRST
         rows = jnp.dot(
             main, recv[q, below : below + width, :], preferred_element_type=jnp.float32
         ).astype(jnp.bfloat16)
@@ -301,7 +307,7 @@
         start, size = (FIRST, CHUNK - FIRST) if h else (0, FIRST)
         return pltpu.make_async_copy(
             part_of(q, 2, h),
-            held.at[pl.ds(q * HELD + 2 * CHUNK + start, size)],
+            held.at[pl.ds(held_row(q, 2) + start, size)],
             own_sem.at[q, h],
         )
 
@@ -324,7 +330,7 @@
         for q in range(NQ):
             for j in range(3):
                 column = jnp.broadcast_to(column_of(keys[j, q], CHUNK), (CHUNK, 128))
-                base = q * HELD + j * CHUNK
+                base = held_row(q, j)
                 key_cols[base : base + CHUNK, :] = column
                 clu_cols[base : base + CHUNK, :] = cluster_of(column)
 
@@ -339,48 +345,13 @@
         for h in range(2):
             arrived(q, 5, h)
 
-    def score(first, count, qq, s):
-        rows = count * HELD
-        scores[0:rows, :] = contract_lanes(
-            held[first * HELD : first * HELD + rows, :], query[qq, s]
-        )
-        key_row = [keys[2 + 2 * s + i, qq] for i in range(2)]
-        clu_row = [cluster_of(row) for row in key_row]
-
-        def one_chunk(k, tops):
-            tops = list(tops)
-            base = pl.multiple_of((first + k) * HELD, 8)
-            for g in range(HELD // 8):
-                at_rows = pl.ds(base + g * 8, 8)
-                from_rows = pl.ds(pl.multiple_of(k * HELD, 8) + g * 8, 8)
-                key_here = key_cols[at_rows, :]
-                clu_here = clu_cols[at_rows, :]
-                top = best_k[at_rows, :]
-                for i in range(2):
-                    value = scores[from_rows, i * 128 : (i + 1) * 128]
-                    value = jnp.where(clu_here == clu_row[i], value, -1.0)
-                    top = jnp.maximum(top, jnp.where(key_row[i] < key_here, value, -1.0))
-                    if CHUNK <= g * 8 < 2 * CHUNK:
-                        tops[i] = jnp.maximum(
-                            tops[i], jnp.where(key_here < key_row[i], value, -1.0)
-                        )
-                best_k[at_rows, :] = top
-            return tuple(tops)
-
-        tops = tuple(best_q[qq, s, :, i * 128 : (i + 1) * 128] for i in range(2))
-        tops = lax.fori_loop(0, count, one_chunk, tops)
-        for i in range(2):
-            best_q[qq, s, :, i * 128 : (i + 1) * 128] = tops[i]
-
-    def score_rows(first, count, qq, s):
-        rows = count * HELD
-        base = pl.multiple_of(first * HELD, 16)
-        scores[0:rows, :] = contract_lanes(held[pl.ds(base, rows), :], query[qq, s])
+    def score(first, rows, qq, s):
+        scores[0:rows, :] = contract_lanes(held[first : first + rows, :], query[qq, s])
         key_row = [keys[2 + 2 * s + i, qq] for i in range(2)]
         clu_row = [cluster_of(row) for row in key_row]
         tops = [best_q[qq, s, :, i * 128 : (i + 1) * 128] for i in range(2)]
         for g in range(rows // 8):
-            at_rows = pl.ds(base + g * 8, 8)
+            at_rows = slice(first + g * 8, first + g * 8 + 8)
             key_here = key_cols[at_rows, :]
             clu_here = clu_cols[at_rows, :]
             top = best_k[at_rows, :]
@@ -388,22 +359,15 @@
                 value = scores[g * 8 : g * 8 + 8, i * 128 : (i + 1) * 128]
                 value = jnp.where(clu_here == clu_row[i], value, -1.0)
                 top = jnp.maximum(top, jnp.where(key_row[i] < key_here, value, -1.0))
-                if CHUNK <= g * 8 % HELD < 2 * CHUNK:
-                    tops[i] = jnp.maximum(tops[i], jnp.where(key_here < key_row[i], value, -1.0))
+                tops[i] = jnp.maximum(tops[i], jnp.where(key_here < key_row[i], value, -1.0))
             best_k[at_rows, :] = top
         for i in range(2):
             best_q[qq, s, :, i * 128 : (i + 1) * 128] = tops[i]
 
-    def score_halves(first, count, start, stop):
+    def score_all(times, pick, *spans):
         def step(t, carry):
-            score(first, count, t // 2, t % 2)
-            return carry
-
-        lax.fori_loop(start, stop, step, 0)
-
-    def score_list(times, pick):
-        def step(t, carry):
-            score_rows(*pick(t))
+            for first, rows in spans:
+                score(first, rows, *pick(t))
             return carry
 
         lax.fori_loop(0, times, step, 0)
@@ -445,31 +409,27 @@
     share(1, 1)
     near(1)
     near(2)
-    score_halves(0, 3, 0, 2)
+    score_all(2, lambda t: (0, t), (0, HELD), (2 * HELD, 2 * HELD))
     share(2, 0)
     cross(3, 0)
     far(1)
     share(2, 1)
     cross(3, 1)
-    score_halves(0, 3, 2, 4)
+    score_all(2, lambda t: (1, t), (0, HELD), (2 * HELD, 4 * CHUNK))
     near(3)
-    score_halves(3, 1, 0, 4)
+    score_all(4, lambda t: (t // 2, t % 2), (HELD, HELD))
     far(2)
     share(3, 0)
-    score_list(4, lambda t: (t % 2 * 2, 2, 2, t // 2))
+    score_all(2, lambda t: (2, t), (0, 4 * CHUNK), (4 * CHUNK, 4 * CHUNK))
     share(3, 1)
-    score_list(2, lambda t: (t * 2, 2, 3, 0))
+    score(0, 2 * HELD, 3, 0)
     far(3)
-    def last(k, carry):
-        score_rows(2 * k, 2, 3, 1)
-        return carry
-
-    lax.fori_loop(0, NQ // 2, last, 0)
+    score(0, 2 * HELD, 3, 1)
 
     square = eye(CHUNK, 128)
 
     def over_query(q, j):
-        base = q * HELD + j * CHUNK
+        base = held_row(q, j)
         column = jnp.max(best_k[base : base + CHUNK, :], axis=1, keepdims=True)
         column = jnp.broadcast_to(column, (CHUNK, 128))
         return jnp.max(jnp.where(square, column, -1.0), axis=0, keepdims=True)
@@ -560,7 +520,7 @@
             pltpu.VMEM((6, NQ, 1, 128), jnp.float32),
             pltpu.VMEM((NQ * HELD, 128), jnp.float32),
             pltpu.VMEM((NQ * HELD, 128), jnp.float32),
-            pltpu.VMEM((NQ * HELD, 256), jnp.float32),
+            pltpu.VMEM((2 * HELD, 256), jnp.float32),
             pltpu.VMEM((NQ * HELD, 128), jnp.float32),
             pltpu.VMEM((NQ, 2, 8, 256), jnp.float32),
             pltpu.VMEM((5, 8, 128), jnp.float32),

time: 72.6 us -> 71.6 us (0.986)
  Pallas kernels: 71.2 us -> 70.2 us
    pallas_call x1, Pallas kernels: 71.2 us -> 70.2 us  [per_device(): pl.pallas_call(kernel, out_shape=jax.ShapeDtypeStruct((1, ROWS), jnp.floa...]
where the time goes in v6:
time: 71.6 us; the launch traced here: 71.5 us
  Pallas kernels  70.2 us (98%)
  local copies, waits for them, and re-layouts  1.22 us (2%)
    pallas_call x1, Pallas kernels, per_device(): pl.pallas_call(kernel, out_shape=jax.ShapeDtypeStruct((1, ROWS), jnp.floa...  70.2 us

profile of v6, /device:TPU:1, one launch (start us, length us, event | category | flops | bytes accessed | tf_op | source)
XLA Modules:
  0.0 71.5 jit_solution(2383841793327123105)
XLA Ops:
  0.0 70.2 %shard_map.37 = f32[1,224]{1,0:T(1,128)} custom-call(bf16[224,1024]{1,0:T(8,128)(2,1)} %emb_hbm.1, s32[1,224]{1,0:T(1,128)} %bitcast.4, s32[1,224]{1,0:T(1,128)} %bitcast.5), custom_call_target="tpu_custom_call" | custom-call | tf_op jit(solution)/shard_map/pallas_call | solution.py:503
  70.2 0.0 copy-start
  70.3 0.7 copy-done
  70.9 0.6 copy.5
Async XLA Ops:
  70.2 0.7 copy-start
